TPU v7x, 32 devices: a whole 2x2x4 slice. The times are simulated.
32 devices in a mesh: wide: 8 (over z, y), narrow: 4 (over x, core).
Axes of the slice: x: 2, y: 2, z: 4, core: 2. Of those that a mesh axis runs over, the one named last changes fastest.
Arguments:
- text_tokens: bfloat16 [256, 256, 512], P(('wide', 'narrow')), may hold values from -6 to 6
- memory: bfloat16 [256, 256, 512], P(('wide', 'narrow')), may hold values from -6 to 6
- cotangent: bfloat16 [256, 256, 512], P(('wide', 'narrow')), may hold values from -6 to 6
- lengths: int32 [256], P(('wide', 'narrow')), may hold values from 1 to 256, as said below
- memory_mask: int32 [256, 256], P(('wide', 'narrow')), may hold values from 0 to 1, as said below
- group_table: int32 [8], replicated, may hold values from 0 to 1, as said below
- self_gain: float32 [512], replicated, may hold values from 0.5 to 1.5
- cross_gain: float32 [512], replicated, may hold values from 0.5 to 1.5
- ffn_gain: float32 [512], replicated, may hold values from 0.5 to 1.5
- self_query: bfloat16 [512, 384], replicated, may hold values from -0.25 to 0.25
- self_key: bfloat16 [512, 384], replicated, may hold values from -0.25 to 0.25
- self_value: bfloat16 [512, 384], replicated, may hold values from -0.25 to 0.25
- self_out: bfloat16 [384, 512], replicated, may hold values from -1.25 to 1.25
- cross_query: bfloat16 [512, 384], replicated, may hold values from -0.25 to 0.25
- cross_key: bfloat16 [512, 384], replicated, may hold values from -0.25 to 0.25
- cross_value: bfloat16 [512, 384], replicated, may hold values from -0.25 to 0.25
- cross_out: bfloat16 [384, 512], replicated, may hold values from -1.25 to 1.25
- ffn_gate: bfloat16 [512, 1024], replicated, may hold values from -0.25 to 0.25
- ffn_up: bfloat16 [512, 1024], replicated, may hold values from -0.25 to 0.25
- ffn_down: bfloat16 [1024, 512], replicated, may hold values from -0.1875 to 0.1875
Outputs:
- layer_output: bfloat16 [256, 256, 512], P(('wide', 'narrow'))
- text_grad: bfloat16 [256, 256, 512], P(('wide', 'narrow'))
- memory_grad: bfloat16 [256, 256, 512], P(('wide', 'narrow'))
- self_gain_grad: float32 [512], replicated
- cross_gain_grad: float32 [512], replicated
- ffn_gain_grad: float32 [512], replicated
- self_query_grad: float32 [512, 384], replicated
- self_key_grad: float32 [512, 384], replicated
- self_value_grad: float32 [512, 384], replicated
- self_out_grad: float32 [384, 512], replicated
- cross_query_grad: float32 [512, 384], replicated
- cross_key_grad: float32 [512, 384], replicated
- cross_value_grad: float32 [512, 384], replicated
- cross_out_grad: float32 [384, 512], replicated
- ffn_gate_grad: float32 [512, 1024], replicated
- ffn_up_grad: float32 [512, 1024], replicated
- ffn_down_grad: float32 [1024, 512], replicated
- group_counts: float32 [2], replicated
Inputs may be any that keep to these rules, and one draw needn't show every extreme that they name: `lengths`: number of leading valid text slots of each item. `memory_mask`: every item has at least one valid memory token. `group_table`: each of the 2 groups holds at least one wide position.
All inputs are finite; a program needn't handle non-finite values.
Results may differ from a plain program's by a relative error of at most 0.02.
The roundings to bfloat16 on the way count: a program that leaves them out, or rounds other values in their place, can miss the bound.
Values sent between devices are 32-bit elements; how exact they have to be, the bound alone decides.
A program may use at most 256 MiB of HBM per device.

v0:
```python
import jax
import jax.numpy as jnp
from jax import lax
from jax.sharding import PartitionSpec as P

HEADS = 6
GROUPS = 2


EPSILON = 1e-06
NEGATIVE = -1e30


def rms_norm(values, gain):
    return values * lax.rsqrt(jnp.mean(values * values, axis=-1, keepdims=True) + EPSILON) * gain


def gelu_product(gate_proj, up_proj):
    return jax.nn.gelu(gate_proj, approximate=True) * up_proj


def project(inputs, weight):
    return jnp.einsum("isd,de->ise", inputs, weight, preferred_element_type=jnp.float32)


def project_back(gradients, weight):
    return jnp.einsum("ise,de->isd", gradients, weight, preferred_element_type=jnp.float32)


def weight_grad(inputs, gradients):
    return jnp.einsum("isd,ise->de", inputs, gradients, preferred_element_type=jnp.float32)


def split_heads(values):
    return values.reshape(values.shape[0], values.shape[1], HEADS, values.shape[2] // HEADS)


def merge_heads(values):
    return values.reshape(values.shape[0], values.shape[1], values.shape[2] * values.shape[3])


def masked_scores(query_heads, key_heads, allowed):
    scaling = query_heads.shape[3] ** (-0.5)
    scores = (
        jnp.einsum("iqhe,ikhe->ihqk", query_heads, key_heads, preferred_element_type=jnp.float32)
        * scaling
    )
    return jnp.where(allowed[:, None], scores, NEGATIVE)


def attend_forward(query_in, key_in, w_query, w_key, w_value, w_out, allowed):
    query_heads = split_heads(project(query_in, w_query).astype(jnp.bfloat16))
    key_heads = split_heads(project(key_in, w_key).astype(jnp.bfloat16))
    value_heads = split_heads(project(key_in, w_value).astype(jnp.bfloat16))
    scores = masked_scores(query_heads, key_heads, allowed)
    maximum = jnp.max(scores, axis=-1, keepdims=True)
    expo_terms = jnp.exp(scores - maximum)
    totals = jnp.sum(expo_terms, axis=-1, keepdims=True)
    probabilities = (expo_terms / totals).astype(jnp.bfloat16)
    mixture = jnp.einsum(
        "ihqk,ikhe->iqhe", probabilities, value_heads, preferred_element_type=jnp.float32
    )
    mixture = merge_heads(mixture).astype(jnp.bfloat16)
    branch = project(mixture, w_out)
    return (branch, (query_heads, key_heads, value_heads, mixture, maximum + jnp.log(totals)))


def attend_backward(
    query_in, key_in, w_query, w_key, w_value, w_out, allowed, kept_state, branch_grad
):
    query_heads, key_heads, value_heads, mixture, log_totals = kept_state
    branch_low = branch_grad.astype(jnp.bfloat16)
    out_grad = weight_grad(mixture, branch_low)
    mixture_grad = jnp.einsum("isd,ed->ise", branch_low, w_out, preferred_element_type=jnp.float32)
    mixture_grad = split_heads(mixture_grad.astype(jnp.bfloat16))
    probabilities = jnp.exp(masked_scores(query_heads, key_heads, allowed) - log_totals)
    value_grad = jnp.einsum(
        "ihqk,iqhe->ikhe",
        probabilities.astype(jnp.bfloat16),
        mixture_grad,
        preferred_element_type=jnp.float32,
    )
    prob_grad = jnp.einsum(
        "iqhe,ikhe->ihqk", mixture_grad, value_heads, preferred_element_type=jnp.float32
    )
    score_grad = probabilities * (
        prob_grad - jnp.sum(probabilities * prob_grad, axis=-1, keepdims=True)
    )
    score_grad = jnp.where(allowed[:, None], score_grad, 0.0).astype(jnp.bfloat16)
    scaling = query_heads.shape[3] ** (-0.5)
    query_grad = (
        jnp.einsum("ihqk,ikhe->iqhe", score_grad, key_heads, preferred_element_type=jnp.float32)
        * scaling
    )
    key_grad = (
        jnp.einsum("ihqk,iqhe->ikhe", score_grad, query_heads, preferred_element_type=jnp.float32)
        * scaling
    )
    query_low = merge_heads(query_grad).astype(jnp.bfloat16)
    key_low = merge_heads(key_grad).astype(jnp.bfloat16)
    value_low = merge_heads(value_grad).astype(jnp.bfloat16)
    weight_grads = (
        weight_grad(query_in, query_low),
        weight_grad(key_in, key_low),
        weight_grad(key_in, value_low),
        out_grad,
    )
    query_in_grad = project_back(query_low, w_query)
    key_in_grad = project_back(key_low, w_key) + project_back(value_low, w_value)
    return (query_in_grad, key_in_grad, weight_grads)


def body(
    text_tokens,
    memory,
    cotangent,
    lengths,
    memory_mask,
    group_table,
    self_gain,
    cross_gain,
    ffn_gain,
    self_query,
    self_key,
    self_value,
    self_out,
    cross_query,
    cross_key,
    cross_value,
    cross_out,
    ffn_gate,
    ffn_up,
    ffn_down,
):
    row_count = text_tokens.shape[1]
    positions = jnp.arange(row_count, dtype=jnp.int32)
    valid_mask = (positions[None, :] < lengths[:, None]).astype(jnp.float32)
    places = jnp.arange(group_table.shape[0], dtype=jnp.int32)
    own_group = jnp.sum(jnp.where(places == lax.axis_index("wide"), group_table, 0))
    one_hot = (jnp.arange(GROUPS, dtype=jnp.int32) == own_group).astype(jnp.float32)
    counts = lax.psum(one_hot * jnp.sum(valid_mask), ("wide", "narrow"))
    root_counts = jnp.sqrt(counts)
    factor = jnp.sum(one_hot * (jnp.sum(counts) / (jnp.sum(root_counts) * root_counts)))
    self_allowed = (positions[None, :, None] >= positions[None, None, :]) & (
        positions[None, None, :] < lengths[:, None, None]
    )
    cross_allowed = (memory_mask > 0)[:, None, :]
    residual = text_tokens.astype(jnp.float32)
    self_input = rms_norm(residual, self_gain).astype(jnp.bfloat16)
    self_branch, self_kept = attend_forward(
        self_input, self_input, self_query, self_key, self_value, self_out, self_allowed
    )
    after_self = residual + self_branch
    cross_input = rms_norm(after_self, cross_gain).astype(jnp.bfloat16)
    cross_branch, cross_kept = attend_forward(
        cross_input, memory, cross_query, cross_key, cross_value, cross_out, cross_allowed
    )
    after_cross = after_self + cross_branch
    ffn_input = rms_norm(after_cross, ffn_gain).astype(jnp.bfloat16)
    gate_proj = project(ffn_input, ffn_gate)
    up_proj = project(ffn_input, ffn_up)
    active = gelu_product(gate_proj, up_proj).astype(jnp.bfloat16)
    layer_output = (after_cross + project(active, ffn_down)).astype(jnp.bfloat16)
    out_grad = cotangent.astype(jnp.float32) * valid_mask[:, :, None]
    down_low = out_grad.astype(jnp.bfloat16)
    down_grad = weight_grad(active, down_low)
    active_grad = jnp.einsum("isd,fd->isf", down_low, ffn_down, preferred_element_type=jnp.float32)
    unused, pullback = jax.vjp(gelu_product, gate_proj, up_proj)
    gate_grad, up_grad = pullback(active_grad)
    gate_low = gate_grad.astype(jnp.bfloat16)
    up_low = up_grad.astype(jnp.bfloat16)
    gate_weight_grad = weight_grad(ffn_input, gate_low)
    up_weight_grad = weight_grad(ffn_input, up_low)
    ffn_input_grad = project_back(gate_low, ffn_gate) + project_back(up_low, ffn_up)
    unused, pullback = jax.vjp(rms_norm, after_cross, ffn_gain)
    norm_grad, ffn_gain_grad = pullback(ffn_input_grad)
    cross_grad = out_grad + norm_grad
    cross_input_grad, memory_raw, cross_weights = attend_backward(
        cross_input,
        memory,
        cross_query,
        cross_key,
        cross_value,
        cross_out,
        cross_allowed,
        cross_kept,
        cross_grad,
    )
    unused, pullback = jax.vjp(rms_norm, after_self, cross_gain)
    norm_grad, cross_gain_grad = pullback(cross_input_grad)
    self_grad = cross_grad + norm_grad
    query_in_grad, key_in_grad, self_weights = attend_backward(
        self_input,
        self_input,
        self_query,
        self_key,
        self_value,
        self_out,
        self_allowed,
        self_kept,
        self_grad,
    )
    unused, pullback = jax.vjp(rms_norm, residual, self_gain)
    norm_grad, self_gain_grad = pullback(query_in_grad + key_in_grad)
    text_raw = self_grad + norm_grad
    text_grad = (factor * text_raw).astype(jnp.bfloat16)
    memory_grad = (factor * memory_raw).astype(jnp.bfloat16)
    gradients = [
        self_gain_grad,
        cross_gain_grad,
        ffn_gain_grad,
        self_weights[0],
        self_weights[1],
        self_weights[2],
        self_weights[3],
        cross_weights[0],
        cross_weights[1],
        cross_weights[2],
        cross_weights[3],
        gate_weight_grad,
        up_weight_grad,
        down_grad,
    ]
    flattened = [entry.reshape(-1) for entry in gradients]
    scaled = [factor * entry for entry in flattened]
    shares = (
        lax.psum_scatter(scaled[0], ("wide", "narrow"), scatter_dimension=0, tiled=True),
        lax.psum_scatter(scaled[1], ("wide", "narrow"), scatter_dimension=0, tiled=True),
        lax.psum_scatter(scaled[2], ("wide", "narrow"), scatter_dimension=0, tiled=True),
        lax.psum_scatter(scaled[3], ("wide", "narrow"), scatter_dimension=0, tiled=True),
        lax.psum_scatter(scaled[4], ("wide", "narrow"), scatter_dimension=0, tiled=True),
        lax.psum_scatter(scaled[5], ("wide", "narrow"), scatter_dimension=0, tiled=True),
        lax.psum_scatter(scaled[6], ("wide", "narrow"), scatter_dimension=0, tiled=True),
        lax.psum_scatter(scaled[7], ("wide", "narrow"), scatter_dimension=0, tiled=True),
        lax.psum_scatter(scaled[8], ("wide", "narrow"), scatter_dimension=0, tiled=True),
        lax.psum_scatter(scaled[9], ("wide", "narrow"), scatter_dimension=0, tiled=True),
        lax.psum_scatter(scaled[10], ("wide", "narrow"), scatter_dimension=0, tiled=True),
        lax.psum_scatter(scaled[11], ("wide", "narrow"), scatter_dimension=0, tiled=True),
        lax.psum_scatter(scaled[12], ("wide", "narrow"), scatter_dimension=0, tiled=True),
        lax.psum_scatter(scaled[13], ("wide", "narrow"), scatter_dimension=0, tiled=True),
    )
    gathered = (
        lax.all_gather(shares[0], ("wide", "narrow"), axis=0, tiled=True),
        lax.all_gather(shares[1], ("wide", "narrow"), axis=0, tiled=True),
        lax.all_gather(shares[2], ("wide", "narrow"), axis=0, tiled=True),
        lax.all_gather(shares[3], ("wide", "narrow"), axis=0, tiled=True),
        lax.all_gather(shares[4], ("wide", "narrow"), axis=0, tiled=True),
        lax.all_gather(shares[5], ("wide", "narrow"), axis=0, tiled=True),
        lax.all_gather(shares[6], ("wide", "narrow"), axis=0, tiled=True),
        lax.all_gather(shares[7], ("wide", "narrow"), axis=0, tiled=True),
        lax.all_gather(shares[8], ("wide", "narrow"), axis=0, tiled=True),
        lax.all_gather(shares[9], ("wide", "narrow"), axis=0, tiled=True),
        lax.all_gather(shares[10], ("wide", "narrow"), axis=0, tiled=True),
        lax.all_gather(shares[11], ("wide", "narrow"), axis=0, tiled=True),
        lax.all_gather(shares[12], ("wide", "narrow"), axis=0, tiled=True),
        lax.all_gather(shares[13], ("wide", "narrow"), axis=0, tiled=True),
    )
    reshaped = [entry.reshape(anchor.shape) for entry, anchor in zip(gathered, gradients)]
    return tuple([layer_output, text_grad, memory_grad] + reshaped + [counts])


def solution(mesh):
    placed = (
        P(("wide", "narrow"), None, None),
        P(("wide", "narrow"), None, None),
        P(("wide", "narrow"), None, None),
        P(("wide", "narrow")),
        P(("wide", "narrow"), None),
        P(),
        P(),
        P(),
        P(),
        P(),
        P(),
        P(),
        P(),
        P(),
        P(),
        P(),
        P(),
        P(),
        P(),
        P(),
    )
    return jax.shard_map(
        body,
        mesh=mesh,
        in_specs=placed,
        out_specs=(
            P(("wide", "narrow"), None, None),
            P(("wide", "narrow"), None, None),
            P(("wide", "narrow"), None, None),
            P(),
            P(),
            P(),
            P(),
            P(),
            P(),
            P(),
            P(),
            P(),
            P(),
            P(),
            P(),
            P(),
            P(),
            P(),
        ),
        check_vma=False,
    )
```

profile of v0, /device:TPU:0, one launch (start us, length us, event | category | flops | bytes accessed | tf_op | source)
XLA Modules:
  0.0 1094.4 jit_solution(15522001949202204953)
XLA Ops:
  12.1 42.0 %psum.7 = f32[2]{0:T(128)S(1)} all-reduce(f32[2]{0:T(128)S(1)} %compare_select_fusion.2), channel_id=1, replica_groups=mesh['wide'=8,'narrow'=4] {'wide','narrow'}, use_global_device_ids=true, to_apply=%region_9.10 | all-reduce | flops 2 | bytes 16 | tf_op jit(solution)/shard_map/psum | solution.py:141
  58.1 4.1 convolution_convert_fusion.6
  62.2 2.6 copy.119
  64.8 4.1 convolution_convert_fusion.5
  68.9 2.6 copy.120
  71.5 4.1 convolution_convert_fusion.7
  75.6 2.6 copy.118
  80.6 2.6 copy.125
  85.5 2.6 copy.123
  88.8 8.7 fusion.13
  97.4 7.9 fusion.4
  106.0 7.1 fusion.110
  116.7 2.5 convolution_convert_fusion.3
  119.1 2.6 copy.124
  121.7 4.7 fusion.14
  126.5 4.6 fusion.5
  131.2 3.9 fusion.111
  138.6 5.7 fusion.135
  144.2 5.7 fusion.139
  149.9 13.5 %multiply_convert_fusion = (bf16[8,256,1024]{2,1,0:T(8,128)(2,1)S(1)}, bf16[8,256,1024]{2,1,0:T(8,128)(2,1)}, bf16[8,256,1024]{2,1,0:T(8,128)(2,1)}) fusion(f32[8,256,1024]{2,1,0:T(8,128)} %fusion.139, f32[8,256,1024]{2,1,0:T(8,128)} %fusion.135, bf16[1024,512]{1,0:T(8,128)(2,1)} %param.39, bf16[8,256,512]{2,1,0:T(8,128)(2,1)S(1)} %copy-done.21, ...), kind=kOutput, calls=%fused_computation.27 | convolution fusion | flops 2205155328 | bytes 32514048 | tf_op jit(solution)/shard_map/isd,fd->isf/dot_general | solution.py:167
  163.4 5.1 fusion.137
  168.5 2.6 fusion.168
  171.1 4.4 fusion.97
  175.4 4.4 fusion.96
  179.8 3.8 multiply_reduce_fusion.2
  185.1 2.5 fusion.131
  190.0 2.8 copy.128
  192.8 8.4 fusion.206
  201.2 7.0 fusion.112
  208.2 23.7 %multiply_convert_fusion.8 = bf16[8,6,64,256]{3,2,1,0:T(8,128)(2,1)} fusion(bf16[8,256,6,64]{1,3,2,0:T(8,128)(2,1)} %bitcast.220, f32[8,6,256,256]{2,3,1,0:T(8,128)} %fusion.206, f32[8,6,256,256]{2,3,1,0:T(8,128)} %copy-done.6, f32[8,6,256]{2,1,0:T(8,128)S(1)} %log_add_fusion.1, pred[8,256]{1,0:T(8,128)(4,1)S(1)} %broadcast_compare_fusion), kind=kOutput, calls=%fused_computation.105 | convolution fusion | flops 438841600 | bytes 28362752 | tf_op jit(solution)/shard_map/ihqk,ikhe->iqhe/dot_general | solution.py:92
  231.9 24.1 %multiply_convert_fusion.5 = bf16[8,6,64,256]{3,2,1,0:T(8,128)(2,1)} fusion(bf16[8,256,6,64]{1,3,2,0:T(8,128)(2,1)} %bitcast.222, f32[8,6,256,256]{2,3,1,0:T(8,128)} %fusion.206, f32[8,6,256,256]{2,3,1,0:T(8,128)} %copy-done.6, f32[8,6,256]{2,1,0:T(8,128)S(1)} %log_add_fusion.1, pred[8,256]{1,0:T(8,128)(4,1)S(1)} %broadcast_compare_fusion), kind=kOutput, calls=%fused_computation.102 | convolution fusion | flops 438841600 | bytes 28362752 | tf_op jit(solution)/shard_map/ihqk,iqhe->ikhe/dot_general | solution.py:96
  256.1 5.6 fusion.125
  265.3 2.6 fusion.124
  270.3 2.6 copy.131
  272.8 8.3 fusion.207
  281.2 8.7 fusion.115
  289.9 20.9 %multiply_convert_fusion.7 = bf16[8,6,64,256]{3,2,1,0:T(8,128)(2,1)} fusion(bf16[8,256,6,64]{1,3,2,0:T(8,128)(2,1)} %bitcast.228, f32[8,6,256,256]{2,3,1,0:T(8,128)} %fusion.207, f32[8,6,256,256]{2,3,1,0:T(8,128)} %get-tuple-element.49, f32[8,6,256]{2,1,0:T(8,128)S(1)} %copy-done.51, pred[8,256,256]{1,2,0:T(8,128)(4,1)S(1)} %broadcast_and_fusion), kind=kOutput, calls=%fused_computation.104 | convolution fusion | flops 438841600 | bytes 28884992 | tf_op jit(solution)/shard_map/ihqk,ikhe->iqhe/dot_general | solution.py:92
  310.8 24.4 %multiply_convert_fusion.6 = bf16[8,6,64,256]{3,2,1,0:T(8,128)(2,1)} fusion(bf16[8,256,6,64]{1,3,2,0:T(8,128)(2,1)} %bitcast.226, f32[8,6,256,256]{2,3,1,0:T(8,128)} %fusion.207, f32[8,6,256,256]{2,3,1,0:T(8,128)} %get-tuple-element.49, f32[8,6,256]{2,1,0:T(8,128)S(1)} %copy-done.51, pred[8,256,256]{1,2,0:T(8,128)(4,1)S(1)} %broadcast_and_fusion), kind=kOutput, calls=%fused_computation.103 | convolution fusion | flops 438841600 | bytes 28884992 | tf_op jit(solution)/shard_map/ihqk,iqhe->ikhe/dot_general | solution.py:96
  335.2 6.0 fusion.95
  347.8 2.5 fusion.129
  355.5 3.9 fusion.127
  364.0 4.4 fusion.122
  369.3 4.4 fusion.120
  374.6 4.4 fusion.121
  380.0 247.3 %all-reduce.22.cloned.1.call-done = (f32[196608]{0:T(1024)}, f32[196608]{0:T(1024)}, f32[196608]{0:T(1024)}, f32[196608]{0:T(1024)}, f32[196608]{0:T(1024)}, /*i...) async-done(((f32[196608]{0:T(1024)}, f32[196608]{0:T(1024)}, f32[196608]{0:T(1024)}, ...) | async-done | bytes 12582928
  630.7 2.8 fusion.157
  635.6 4.3 fusion.86
  641.2 39.7 %all-reduce.18 = (f32[512]{0:T(512)S(1)}, f32[512]{0:T(512)S(1)}, f32[512]{0:T(512)S(1)}) all-reduce(f32[512]{0:T(512)S(1)} %broadcast_multiply_fusion.2, f32[512]{0:T(512)S(1)} %get-tuple-element.60, f32[512]{0:T(512)S(1)} %get-tuple-element.59), channel_id=2, replica_groups=mesh['wide'=8,'narrow'=4] {'wide','narrow'}, use_global_device_ids=true, to_apply=%region_19.20.clone | all-reduce | flops 1536 | bytes 12288
  681.4 39.8 %all-reduce.17 = (f32[512]{0:T(512)}, f32[512]{0:T(512)}, f32[512]{0:T(512)}) all-reduce(f32[512]{0:T(512)S(1)} %dynamic-slice_dynamic-update-slice_fusion.2, f32[512]{0:T(512)S(1)} %dynamic-slice_dynamic-update-slice_fusion.1, f32[512]{0:T(512)S(1)} %dynamic-slice_dynamic-update-slice_fusion), channel_id=1, replica_groups=mesh['wide'=8,'narrow'=4] {'wide','narrow'}, use_global_device_ids=true, to_apply=%add | all-reduce | flops 1536 | bytes 12288
  721.2 4.8 fusion.147
  726.0 5.2 fusion.91
  732.8 6.5 multiply_convert_fusion.2
  739.3 5.9 add_convert_fusion
  751.1 43.9 %all_gather.52 = f32[196608]{0:T(1024)S(1)} all-gather(f32[6144]{0:T(1024)S(1)} %dynamic-slice.10), channel_id=1, replica_groups=mesh['wide'=8,'narrow'=4] {'wide','narrow'}, dimensions={0}, use_global_device_ids=true | all-gather | bytes 811008 | tf_op jit(solution)/shard_map/all_gather | solution.py:253
  795.9 39.4 %all_gather.51 = f32[196608]{0:T(1024)S(1)} all-gather(f32[6144]{0:T(1024)S(1)} %dynamic-slice.9), channel_id=1, replica_groups=mesh['wide'=8,'narrow'=4] {'wide','narrow'}, dimensions={0}, use_global_device_ids=true | all-gather | bytes 811008 | tf_op jit(solution)/shard_map/all_gather | solution.py:252
  836.4 39.8 %all_gather.50 = f32[196608]{0:T(1024)S(1)} all-gather(f32[6144]{0:T(1024)S(1)} %dynamic-slice.8), channel_id=1, replica_groups=mesh['wide'=8,'narrow'=4] {'wide','narrow'}, dimensions={0}, use_global_device_ids=true | all-gather | bytes 811008 | tf_op jit(solution)/shard_map/all_gather | solution.py:251
  877.3 39.0 %all_gather.49 = f32[196608]{0:T(1024)S(1)} all-gather(f32[6144]{0:T(1024)S(1)} %dynamic-slice.7), channel_id=1, replica_groups=mesh['wide'=8,'narrow'=4] {'wide','narrow'}, dimensions={0}, use_global_device_ids=true | all-gather | bytes 811008 | tf_op jit(solution)/shard_map/all_gather | solution.py:250
  917.4 39.8 %all_gather.48 = f32[196608]{0:T(1024)S(1)} all-gather(f32[6144]{0:T(1024)S(1)} %dynamic-slice.6), channel_id=1, replica_groups=mesh['wide'=8,'narrow'=4] {'wide','narrow'}, dimensions={0}, use_global_device_ids=true | all-gather | bytes 811008 | tf_op jit(solution)/shard_map/all_gather | solution.py:249
  958.2 39.0 %all_gather.47 = f32[196608]{0:T(1024)S(1)} all-gather(f32[6144]{0:T(1024)S(1)} %dynamic-slice.5), channel_id=1, replica_groups=mesh['wide'=8,'narrow'=4] {'wide','narrow'}, dimensions={0}, use_global_device_ids=true | all-gather | bytes 811008 | tf_op jit(solution)/shard_map/all_gather | solution.py:248
  998.3 39.8 %all_gather.46 = f32[196608]{0:T(1024)S(1)} all-gather(f32[6144]{0:T(1024)S(1)} %dynamic-slice.4), channel_id=1, replica_groups=mesh['wide'=8,'narrow'=4] {'wide','narrow'}, dimensions={0}, use_global_device_ids=true | all-gather | bytes 811008 | tf_op jit(solution)/shard_map/all_gather | solution.py:247
  1039.1 39.0 %all_gather.45 = f32[196608]{0:T(1024)S(1)} all-gather(f32[6144]{0:T(1024)S(1)} %dynamic-slice.3), channel_id=1, replica_groups=mesh['wide'=8,'narrow'=4] {'wide','narrow'}, dimensions={0}, use_global_device_ids=true | all-gather | bytes 811008 | tf_op jit(solution)/shard_map/all_gather | solution.py:246
  1079.2 2.7 reshape.299
  1081.9 2.7 reshape.301
  1084.7 2.7 reshape.300
  (195 shorter events, 74.1 us)
Async XLA Ops:
  7.2 71.0 %copy-start = (bf16[8,256,512]{2,1,0:T(8,128)(2,1)S(1)}, bf16[8,256,512]{2,1,0:T(8,128)(2,1)}, u32[]{:S(2)}) copy-start(bf16[8,256,512]{2,1,0:T(8,128)(2,1)} %param.21) | copy-start | bytes 6291460
  7.2 620.1 %all-reduce.22.cloned.1.call-start = ((), (), s32[]{:S(2)}) async-start(), calls=%async_computation.3 | async-start | bytes 25165824
  54.1 114.4 %copy-start.55 = (f32[2]{0:T(128)}, f32[2]{0:T(128)S(1)}, u32[]{:S(2)}) copy-start(f32[2]{0:T(128)S(1)} %psum.7) | copy-start | bytes 28
  57.5 0.6 copy-start.47
  58.1 13.4 %copy-start.49 = (f32[8,256]{1,0:T(8,128)}, f32[8,256]{1,0:T(8,128)S(1)}, u32[]{:S(2)}) copy-start(f32[8,256]{1,0:T(8,128)S(1)} %fusion.165) | copy-start | bytes 24580
  58.1 6.7 copy-start.39
  58.1 6.7 copy-start.53
  64.8 6.7 copy-start.44
  71.5 6.7 copy-start.42
  78.2 5.0 copy-start.37
  97.4 8.6 copy-start.17
  106.0 7.1 copy-start.11
  106.0 7.1 copy-start.25
  113.1 1.6 copy-start.28
  113.1 3.6 copy-start.23
  113.1 3.6 copy-start.46
  114.6 2.1 copy-start.1
  126.5 4.7 copy-start.6
  126.5 4.7 copy-start.18
  131.2 3.9 copy-start.2
  131.2 3.9 copy-start.22
  135.1 1.4 copy-start.31
  135.1 1.5 copy-start.52
  136.5 47.1 %copy-start.4 = (f32[8,256,512]{2,1,0:T(8,128)}, f32[8,256,512]{2,1,0:T(8,128)S(1)}, u32[]{:S(2)}) copy-start(f32[8,256,512]{2,1,0:T(8,128)S(1)} %get-tuple-element.55) | copy-start | bytes 12582916
  136.5 2.0 copy-start.34
  138.6 5.7 copy-start.56
  144.2 5.7 copy-start.21
  163.4 7.7 copy-start.15
  175.4 4.4 copy-start.35
  183.6 1.4 copy-start.32
  185.1 2.5 copy-start.9
  192.8 8.4 copy-start.19
  256.0 5.6 copy-start.3
  256.0 5.6 copy-start.16
  256.0 5.6 copy-start.24
  261.6 2.2 copy-start.10
  263.9 1.4 copy-start.29
  265.3 2.6 copy-start.7
  265.3 2.6 copy-start.26
  272.8 8.3 copy-start.20
  272.8 8.3 copy-start.51
  335.2 6.0 copy-start.36
  341.2 3.0 copy-start.13
  342.3 3.7 copy-start.14
  344.2 3.6 copy-start.27
  355.5 8.5 copy-start.50
  355.5 8.5 copy-start.54
  379.9 250.7 %copy-start.40 = (bf16[512,384]{1,0:T(8,128)(2,1)S(1)}, bf16[512,384]{1,0:T(8,128)(2,1)}, u32[]{:S(2)}) copy-start(bf16[512,384]{1,0:T(8,128)(2,1)} %param.30) | copy-start | bytes 1179652
  379.9 253.6 %copy-start.41 = (bf16[512,384]{1,0:T(8,128)(2,1)S(1)}, bf16[512,384]{1,0:T(8,128)(2,1)}, u32[]{:S(2)}) copy-start(bf16[512,384]{1,0:T(8,128)(2,1)} %param.29) | copy-start | bytes 1179652
  380.0 699.3 %all-gather.4.cloned.1.call-start = ((), (), s32[]{:S(2)}) async-start(), calls=%async_computation | async-start | bytes 2162688 | tf_op jit(solution)/shard_map/all_gather | solution.py:254
  628.8 453.2 %all-gather.8.cloned.1.call-start = ((), (), s32[]{:S(2)}) async-start(), calls=%async_computation.2 | async-start | bytes 2162688 | tf_op jit(solution)/shard_map/all_gather | solution.py:256
  630.3 454.3 %all-gather.6.cloned.1.call-start = ((), (), s32[]{:S(2)}) async-start(), calls=%async_computation.1 | async-start | bytes 2162688 | tf_op jit(solution)/shard_map/all_gather | solution.py:255
  630.6 2.9 copy-start.30
  633.5 1.6 copy-start.12
  633.5 2.0 copy-start.33
  633.5 2.1 copy-start.45
  635.6 85.6 %copy-start.48 = (f32[8,256]{1,0:T(8,128)S(1)}, f32[8,256]{1,0:T(8,128)}, u32[]{:S(2)}) copy-start(f32[8,256]{1,0:T(8,128)} %copy-done.47) | copy-start | bytes 24580
  635.6 85.6 %copy-start.43 = (bf16[512,384]{1,0:T(8,128)(2,1)S(1)}, bf16[512,384]{1,0:T(8,128)(2,1)}, u32[]{:S(2)}) copy-start(bf16[512,384]{1,0:T(8,128)(2,1)} %param.34) | copy-start | bytes 1179652
  721.2 4.8 copy-start.8
  726.0 6.7 copy-start.38
  732.7 6.6 copy-start.57
  732.8 6.5 copy-start.5
Sparse Core Ops, SparseCore 0:
  380.1 247.1 all-reduce.21
  630.7 56.1 all-gather.3
  689.7 55.5 all-gather.7
  748.6 56.8 all-gather.5
where the time goes:
time: 1100 us; the launch traced here: 1090 us
  blocking collectives  441 us (40%)
  matrix products  284 us (26%)
  waiting for transfers between devices  247 us (22%)
  local copies, waits for them, and re-layouts  72.8 us (7%)
  other arithmetic  34 us (3%)
  between operations  15 us (1%)
    unnamed x5, waiting for transfers between devices  247 us
    unnamed x2, blocking collectives  79.5 us
    dot_general x2, matrix products, attend_backward(): jnp.einsum('ihqk,iqhe->ikhe', score_grad, query_heads, preferred_element_...  48.6 us
    dot_general x11, matrix products, weight_grad(): jnp.einsum('isd,ise->de', inputs, gradients, preferred_element_type=jnp.f...  44.9 us
    dot_general x2, matrix products, attend_backward(): jnp.einsum('ihqk,ikhe->iqhe', score_grad, key_heads, preferred_element_ty...  44.6 us
    all_gather x1, blocking collectives, body(): lax.all_gather(shares[10], ('wide', 'narrow'), axis=0, tiled=True)  43.9 us
    psum x1, blocking collectives, body(): counts = lax.psum(one_hot * jnp.sum(valid_mask), ('wide', 'narrow'))  42 us
    all_gather x1, blocking collectives, body(): lax.all_gather(shares[6], ('wide', 'narrow'), axis=0, tiled=True)  39.8 us
  transfers between devices with their start and end apart: 4, of which 1 were waited for; matrix products, arithmetic and copies ran while one was open for 5% of the time, Pallas kernels for 0%

commit v1 on v0

v1 whole, which is shorter than its diff:
```python
import functools

import jax
import jax.numpy as jnp
from jax import lax
from jax.experimental import pallas as pl
from jax.experimental.pallas import tpu as pltpu
from jax.sharding import PartitionSpec as P

HEADS = 6
GROUPS = 2
EPSILON = 1e-06
NEGATIVE = -1e30
F32 = jnp.float32
BF16 = jnp.bfloat16
AXES = ("wide", "narrow")
ROOT = 0.7978845608028654
CUBE = 0.044715
MIB = 1 << 20


def contract(left, right, left_dim, right_dim):
    return lax.dot_general(
        left, right, (((left_dim,), (right_dim,)), ((), ())), preferred_element_type=F32
    )


def nn(left, right):
    return contract(left, right, 1, 0)


def nt(left, right):
    return contract(left, right, 1, 1)


def tn(left, right):
    return contract(left, right, 0, 0)


def norm_scale(values):
    return lax.rsqrt(jnp.mean(values * values, axis=-1, keepdims=True) + EPSILON)


def norm_back(values, gain, grad):
    scale = norm_scale(values)
    unit = values * scale
    gain_rows = grad * unit
    dot = jnp.mean(gain_rows * gain, axis=-1, keepdims=True)
    return scale * (grad * gain - unit * dot), jnp.sum(gain_rows, axis=0, keepdims=True)


def low_lanes(rows):
    return lax.broadcasted_iota(jnp.int32, (rows, 128), 1) < 64


def stack_heads(pair, low):
    zero = jnp.zeros_like(pair)
    return jnp.concatenate([jnp.where(low, pair, zero), jnp.where(low, zero, pair)], axis=0)


def pick_heads(stacked, low):
    rows = stacked.shape[0] // 2
    return jnp.where(low, stacked[:rows], stacked[rows:])


def pair_slice(values, index):
    return values[:, 128 * index : 128 * index + 128]


def attend(query, key, value, mask, qkv_ref, prob_ref, mix_ref):
    rows = query.shape[0]
    low = low_lanes(rows)
    query = (query * 0.125).astype(BF16)
    key = key.astype(BF16)
    value = value.astype(BF16)
    mixed = []
    for j in range(HEADS // 2):
        q, k, v = pair_slice(query, j), pair_slice(key, j), pair_slice(value, j)
        qkv_ref[j, 0, :, 0:128] = q
        qkv_ref[j, 0, :, 128:256] = k
        qkv_ref[j, 0, :, 256:384] = v
        scores = mask(nt(stack_heads(q, low), k))
        top = jnp.max(scores, axis=-1, keepdims=True)
        expo = jnp.exp(scores - top)
        total = jnp.sum(expo, axis=-1, keepdims=True)
        prob = (expo * (1.0 / total)).astype(BF16)
        prob_ref[j, 0] = prob
        mixed.append(pick_heads(nn(prob, v), low))
    mixture = jnp.concatenate(mixed, axis=1).astype(BF16)
    mix_ref[0] = mixture
    return mixture


def forward_kernel(
    len_ref, text_ref, mem_ref, mask_ref, self_gain, cross_gain, ffn_gain,
    sq_ref, sk_ref, sv_ref, so_ref, cq_ref, ck_ref, cv_ref, co_ref,
    sqkv_ref, sprob_ref, smix_ref, mid_ref, cin_ref, cqkv_ref, cprob_ref, cmix_ref, post_ref, fin_ref,
    wqkv, wkv,
):
    item = pl.program_id(0)
    inner = sq_ref.shape[1]

    @pl.when(item == 0)
    def _():
        wqkv[:, :inner] = sq_ref[...]
        wqkv[:, inner : 2 * inner] = sk_ref[...]
        wqkv[:, 2 * inner :] = sv_ref[...]
        wkv[:, :inner] = ck_ref[...]
        wkv[:, inner:] = cv_ref[...]

    rows = text_ref.shape[1]
    length = len_ref[item]
    row = lax.broadcasted_iota(jnp.int32, (2 * rows, rows), 0)
    row = jnp.where(row >= rows, row - rows, row)
    col = lax.broadcasted_iota(jnp.int32, (2 * rows, rows), 1)
    allowed = (col <= row) & (col < length)
    text = text_ref[0].astype(F32)
    self_in = (text * norm_scale(text) * self_gain[...]).astype(BF16)
    proj = nn(self_in, wqkv[...])
    mixture = attend(
        proj[:, :inner], proj[:, inner : 2 * inner], proj[:, 2 * inner :],
        lambda s: jnp.where(allowed, s, NEGATIVE), sqkv_ref, sprob_ref, smix_ref,
    )
    mid = text + nn(mixture, so_ref[...])
    mid_ref[0] = mid
    cross_in = (mid * norm_scale(mid) * cross_gain[...]).astype(BF16)
    cin_ref[0] = cross_in
    query = nn(cross_in, cq_ref[...])
    proj = nn(mem_ref[0], wkv[...])
    open_keys = mask_ref[pl.ds(item, 1), :] > 0
    mixture = attend(
        query, proj[:, :inner], proj[:, inner:],
        lambda s: jnp.where(open_keys, s, NEGATIVE), cqkv_ref, cprob_ref, cmix_ref,
    )
    post = mid + nn(mixture, co_ref[...])
    post_ref[0] = post
    fin_ref[0] = (post * norm_scale(post) * ffn_gain[...]).astype(BF16)


def forward(lengths, text, memory, mask, gains, weights):
    items, rows, width = text.shape
    inner = weights[0].shape[1]
    pairs = HEADS // 2

    def whole(array):
        zeros = (0,) * array.ndim
        return pl.BlockSpec(array.shape, lambda i: zeros)

    def per_item(*shape):
        zeros = (0,) * len(shape)
        return pl.BlockSpec((1,) + shape, lambda i: (i,) + zeros)

    def per_pair(*shape):
        return pl.BlockSpec((pairs, 1) + shape, lambda i: (0, i, 0, 0))

    qkv_shape = jax.ShapeDtypeStruct((pairs, items, rows, 384), BF16)
    prob_shape = jax.ShapeDtypeStruct((pairs, items, 2 * rows, rows), BF16)
    mix_shape = jax.ShapeDtypeStruct((items, rows, inner), BF16)
    full_shape = jax.ShapeDtypeStruct((items, rows, width), F32)
    half_shape = jax.ShapeDtypeStruct((items, rows, width), BF16)
    qkv_spec, prob_spec = per_pair(rows, 384), per_pair(2 * rows, rows)
    mix_spec, row_spec = per_item(rows, inner), per_item(rows, width)
    return pl.pallas_call(
        forward_kernel,
        grid=(items,),
        in_specs=[pl.BlockSpec(memory_space=pltpu.SMEM), row_spec, row_spec, whole(mask)]
        + [whole(g) for g in gains]
        + [whole(w) for w in weights],
        out_specs=[qkv_spec, prob_spec, mix_spec, row_spec, row_spec, qkv_spec, prob_spec, mix_spec, row_spec, row_spec],
        out_shape=[qkv_shape, prob_shape, mix_shape, full_shape, half_shape, qkv_shape, prob_shape, mix_shape, full_shape, half_shape],
        scratch_shapes=[pltpu.VMEM((width, 3 * inner), BF16), pltpu.VMEM((width, 2 * inner), BF16)],
        compiler_params=pltpu.CompilerParams(vmem_limit_bytes=63 * MIB),
        name="forward",
    )(lengths, text, memory, mask, *gains, *weights)


RISE = (0, 1, 3, 5, 6, 8, 9, 11, 13, 15)
HALVES = 5
LEGS = 2 * HALVES - 1


def exchange_plan():
    wide, narrow = lax.axis_index("wide"), lax.axis_index("narrow")
    z, y = wide // 2, wide % 2
    x, core = narrow // 2, narrow % 2
    near, far = z % 2, z // 2
    flip_x = (wide, (1 - x) * 2 + core)
    flip_y = (z * 2 + 1 - y, narrow)
    flip_core = (wide, x * 2 + 1 - core)
    flip_near = ((far * 2 + 1 - near) * 2 + y, narrow)
    flip_far = (((1 - far) * 2 + near) * 2 + y, narrow)

    def choose(first, second):
        return first + core * (second - first)

    first_flip = tuple(choose(a, b) for a, b in zip(flip_x, flip_y))
    third_flip = tuple(choose(b, a) for a, b in zip(flip_x, flip_y))
    bits = (core, choose(x, y), near, choose(y, x), far)
    partners = (flip_core, first_flip, flip_near, third_flip, flip_far)
    plain = (flip_core, flip_x, flip_near, flip_y, flip_far)
    return bits, partners, plain


def backward_kernel(
    linked, items, rows, width, inner, hidden,
    len_ref, group_ref, self_gain, cross_gain, ffn_gain,
    fin_hbm, cot_hbm, gate_hbm, up_hbm, down_hbm, post_hbm,
    cqkv_hbm, cprob_hbm, cmix_hbm, cq_hbm, ck_hbm, cv_hbm, co_hbm, cin_hbm, mem_hbm, mid_hbm,
    sqkv_hbm, sprob_hbm, smix_hbm, sq_hbm, sk_hbm, sv_hbm, so_hbm, text_hbm,
    out_hbm, text_grad_hbm, mem_grad_hbm, *rest,
):
    if linked:
        outs, rest = rest[:11], rest[11:]
        gain_grads, counts_ref, grads = rest[0], rest[1], rest[2]
        halves, small, small_in, factor_ref, send_sem, recv_sem, small_send, small_recv, done_sem, free_sem = rest[3:13]
        rest = rest[13:]
    else:
        grads, gain_grads = rest[:2]
        rest = rest[2:]
    (xf, din, first, second, first_t, second_t, gate, up, down, work,
    wqkv, wout, qkv, prob, mix, dmix, stage, load_sem, out_sem) = rest
    pairs = HEADS // 2
    chunk = 256
    chunks = hidden // chunk
    low = low_lanes(rows)
    units = 2 * chunks + 2 * (1 + pairs)
    last_tick = 2 * (units - 1) + RISE[-1]
    if linked:
        bits, partners, plain = exchange_plan()
        barrier = pltpu.get_barrier_semaphore()
        for device in (plain[0], plain[1], plain[2], plain[3], plain[4]):
            pl.semaphore_signal(barrier, inc=1, device_id=device, device_id_type=pl.DeviceIdType.MESH)
        pl.semaphore_wait(barrier, len(plain))

    half = 3 * width // 2

    def region(step, own):
        start = 0
        for s in range(step + 1):
            bit = bits[s] if own or s < step else 1 - bits[s]
            start = start + bit * (half >> s)
        return pl.ds(pl.multiple_of(start, 16), half >> step)

    def half_rows(step):
        size = half >> min(step, HALVES - 2)
        return pl.ds(2 * half - (2 * half >> step), size)

    def stage_copy(index, k):
        slot = k % 2 if isinstance(k, int) else lax.rem(k, 2)
        if index < HALVES:
            sent = region(index, False) if index < HALVES - 1 else region(HALVES - 2, True)
            source, target = grads.at[k, sent], halves.at[slot, half_rows(index)]
            step = index
        else:
            step = LEGS - 1 - index
            source = target = grads.at[k, region(step, True)]
        return pltpu.make_async_remote_copy(
            src_ref=source, dst_ref=target, send_sem=send_sem.at[slot, index], recv_sem=recv_sem.at[slot, index],
            device_id=partners[step], device_id_type=pl.DeviceIdType.MESH,
        )

    def result_copies(k):
        return [
            pltpu.make_async_copy(
                grads.at[k, pl.ds(start, count), :], outs[out].at[pl.ds(row, count), pl.ds(col, 128)], done_sem.at[k, n]
            )
            for n, (out, row, col, unit, start, count) in enumerate(
                entry for entry in unpack_blocks(width, inner, hidden) if entry[3] == k
            )
        ]

    def advance(index, k):
        slot = k % 2 if isinstance(k, int) else lax.rem(k, 2)
        if index > 0:
            stage_copy(index - 1, k).wait()
        if 0 < index <= HALVES:
            step = min(index - 1, HALVES - 2)
            own = region(step, True)
            value = grads[k, own, :] + halves[slot, half_rows(index - 1), :]
            if index == 1:
                value = value * factor_ref[0:1, :]
            grads[k, own, :] = value
            if index < HALVES:
                pl.semaphore_signal(
                    free_sem.at[k, step], inc=1, device_id=partners[step], device_id_type=pl.DeviceIdType.MESH
                )
        if index < LEGS:
            if index >= HALVES:
                pl.semaphore_wait(free_sem.at[k, LEGS - 1 - index], 1)
            stage_copy(index, k).start()
        else:
            for copy in result_copies(k):
                copy.start()

    def tick(t):
        if not linked:
            return
        for index in reversed(range(LEGS + 1)):
            u = t - RISE[index]
            if isinstance(t, int):
                if u >= 0 and u % 2 == 0 and u < 2 * units:
                    advance(index, u // 2)
            elif index < LEGS:
                ready = (u >= 0) & (u < 2 * units) & (lax.rem(u + 32, 2) == 0)
                pl.when(ready)(functools.partial(advance, index, u // 2))

    def small_copy(use, step):
        return pltpu.make_async_remote_copy(
            src_ref=small.at[use, step], dst_ref=small_in.at[use, step],
            send_sem=small_send.at[use, step], recv_sem=small_recv.at[use, step],
            device_id=plain[step], device_id_type=pl.DeviceIdType.MESH,
        )

    def small_step(use, step):
        if not linked:
            return
        if step > 0:
            small_copy(use, step - 1).wait()
            small[use, step] = small[use, step - 1] + small_in[use, step - 1]
        if step < HALVES:
            small_copy(use, step).start()

    if linked:
        total = len_ref[0]
        for i in range(1, items):
            total = total + len_ref[i]
        lane = lax.broadcasted_iota(jnp.int32, (8, width), 1)
        small[0, 0] = jnp.where(lane == group_ref[lax.axis_index("wide")], total.astype(F32), 0.0)
        small_step(0, 0)

    def set_factor():
        if not linked:
            return
        counts = small[0, HALVES]
        lane = lax.broadcasted_iota(jnp.int32, (8, width), 1)
        counts_ref[...] = counts[:, 0:128]
        roots = jnp.sqrt(counts)
        own = jnp.sum(jnp.where(lane == group_ref[lax.axis_index("wide")], roots, 0.0), axis=-1, keepdims=True)
        top = jnp.sum(counts, axis=-1, keepdims=True)
        bottom = jnp.sum(roots, axis=-1, keepdims=True) * own
        factor_ref[...] = jnp.broadcast_to(top / bottom, (8, 128))

    def scaled(values):
        if linked:
            return values * factor_ref[0:1, 0:1]
        return values * group_ref[0]

    def load(index, source, target):
        return pltpu.make_async_copy(source, target, load_sem.at[index])

    def weights(base, which, query, key, value, out):
        return [
            load(base, query, wqkv.at[which, :, pl.ds(0, inner)]),
            load(base + 1, key, wqkv.at[which, :, pl.ds(inner, inner)]),
            load(base + 2, value, wqkv.at[which, :, pl.ds(2 * inner, inner)]),
            load(base + 3, out, wout.at[which]),
        ]

    fin_load = load(0, fin_hbm, first)
    cot_load = load(1, cot_hbm, second)
    ffn_loads = [load(2, gate_hbm, gate), load(3, up_hbm, up), load(4, down_hbm, down)]
    post_load = load(5, post_hbm, xf)
    cross_weights = weights(6, 0, cq_hbm, ck_hbm, cv_hbm, co_hbm)
    self_weights = weights(10, 1, sq_hbm, sk_hbm, sv_hbm, so_hbm)
    cqkv_loads = [load(14 + j, cqkv_hbm.at[j], qkv.at[j]) for j in range(pairs)]
    cprob_loads = [load(17 + j, cprob_hbm.at[j], prob.at[j]) for j in range(pairs)]
    cmix_load = load(20, cmix_hbm, mix)
    early = [fin_load, cot_load] + ffn_loads + [post_load] + cross_weights + [cmix_load]
    for copy in early + cqkv_loads + cprob_loads + self_weights:
        copy.start()

    def item_rows(i):
        return pl.ds(pl.multiple_of(i * rows, rows), rows)

    def each_item(body, start=0, stop=items):
        def step(i, carry):
            body(i)
            return carry

        lax.fori_loop(start, stop, step, 0)

    middle = items // 2

    def emit(i, values, target):
        slot = lax.rem(i, 2)
        copy = pltpu.make_async_copy(stage.at[slot], target.at[i], out_sem.at[slot])

        @pl.when(i >= 2)
        def _():
            copy.wait()

        stage[slot] = values
        copy.start()

    def drain(target):
        for slot in range(2):
            pltpu.make_async_copy(stage.at[slot], target.at[items - 2 + slot], out_sem.at[slot]).wait()

    fin_load.wait()
    cot_load.wait()
    gain_grads[...] = jnp.zeros_like(gain_grads)

    def prepare(i):
        row = lax.broadcasted_iota(jnp.int32, (rows, width), 0)
        masked = jnp.where(row < len_ref[i], second[i], jnp.zeros((), BF16))
        second[i] = masked
        first_t[:, item_rows(i)] = first[i].T
        second_t[:, item_rows(i)] = masked.T
        din[i] = jnp.zeros((rows, width), F32)

    bounds = [items * s // (HALVES - 1) for s in range(HALVES)]
    for s in range(HALVES - 1):
        each_item(prepare, bounds[s], bounds[s + 1])
        small_step(0, s + 1)
    for copy in ffn_loads:
        copy.wait()
    post_load.wait()
    small_step(0, HALVES)
    set_factor()

    def ffn_chunk(c, carry):
        cols = pl.ds(pl.multiple_of(c * chunk, chunk), chunk)
        wg, wu, wd = gate.at[:, cols], up.at[:, cols], down.at[cols, :]

        def elementwise(i):
            source = first[i]
            g = nn(source, wg[...])
            u = nn(source, wu[...])
            dh = nt(second[i], wd[...])
            square = g * g
            t = jnp.tanh(g * (ROOT + (ROOT * CUBE) * square))
            cdf = 0.5 + 0.5 * t
            act = g * cdf
            slope = cdf + 0.5 * g * (1.0 - t * t) * (ROOT + (3.0 * ROOT * CUBE) * square)
            work[item_rows(i), 0:chunk] = (dh * u * slope).astype(BF16)
            work[item_rows(i), chunk : 2 * chunk] = (dh * act).astype(BF16)
            work[item_rows(i), 2 * chunk : 3 * chunk] = (act * u).astype(BF16)

        each_item(elementwise, 0, middle)
        tick(4 * c - 1)
        each_item(elementwise, middle, items)
        both = nn(first_t[...], work[:, 0 : 2 * chunk])
        turned = nn(second_t[...], work[:, 2 * chunk : 3 * chunk])
        for h in range(chunk // 128):
            place = (chunk // 128) * c + h
            grads[place, 0:width, :] = pair_slice(both, h)
            grads[place, width : 2 * width, :] = pair_slice(both, chunk // 128 + h)
            for m in range(width // 128):
                grads[place, 2 * width + 128 * m : 2 * width + 128 * m + 128, :] = (
                    turned[128 * m : 128 * m + 128, 128 * h : 128 * h + 128].T
                )

        tick(4 * c)

        def spread(i):
            xf[i] += nn(work[item_rows(i), 2 * chunk : 3 * chunk], wd[...])
            din[i] += nt(work[item_rows(i), 0:chunk], wg[...]) + nt(
                work[item_rows(i), chunk : 2 * chunk], wu[...]
            )

        each_item(spread, 0, middle)
        tick(4 * c + 1)
        each_item(spread, middle, items)
        tick(4 * c + 2)
        return carry

    lax.fori_loop(0, chunks, ffn_chunk, 0)
    cin_load = load(0, cin_hbm, first)
    cin_load.start()
    mem_loads = [
        load(21 + i, mem_hbm.at[i], work.at[pl.ds(i * rows, rows), pl.ds(0, width)]) for i in range(items)
    ]
    for copy in mem_loads:
        copy.start()
    each_item(lambda i: emit(i, xf[i].astype(BF16), out_hbm))
    drain(out_hbm)
    clock = 4 * chunks - 1
    tick(clock)
    post_load.start()
    cin_load.wait()
    for copy in mem_loads + cross_weights:
        copy.wait()
    cmix_load.wait()
    post_load.wait()

    def add_out_grad(place, i, branch):
        product = tn(mix[i], branch)
        for m in range(width // 128):
            grads[place, inner * m : inner * m + inner, :] += pair_slice(product, m)

    base = 2 * chunks
    grads[base] = jnp.zeros_like(grads[base])

    def cross_start(i):
        back, gain_rows = norm_back(xf[i], ffn_gain[...], din[i])
        gain_grads[2:3] += gain_rows
        total = second[i].astype(F32) + back
        din[i] = total
        branch = total.astype(BF16)
        dmix[i] = nt(branch, wout[0]).astype(BF16)
        add_out_grad(base, i, branch)
        first_t[:, item_rows(i)] = first[i].T
        second_t[:, item_rows(i)] = work[item_rows(i), 0:width].T

    each_item(cross_start)
    clock += 1
    tick(clock)
    mid_load = load(5, mid_hbm, xf)
    mid_load.start()
    text_load = load(0, text_hbm, first)
    text_load.start()

    def pair_back(j, i):
        lanes = pl.ds(pl.multiple_of(j * 128, 128), 128)
        q, k, v = qkv[j, i, :, 0:128], qkv[j, i, :, 128:256], qkv[j, i, :, 256:384]
        chance = prob[j, i]
        grad = dmix[i, :, lanes]
        product = grad.astype(F32) * mix[i, :, lanes].astype(F32)
        sums = jnp.sum(stack_heads(product, low), axis=-1, keepdims=True)
        grad2 = stack_heads(grad, low)
        score_grad = (chance.astype(F32) * (nt(grad2, v) - sums)).astype(BF16)
        dq = pick_heads(nn(score_grad, k), low) * 0.125
        work[item_rows(i), lanes] = dq.astype(BF16)
        work[item_rows(i), pl.ds(pl.multiple_of(inner + j * 128, 128), 128)] = tn(
            score_grad, stack_heads(q, low)
        ).astype(BF16)
        work[item_rows(i), pl.ds(pl.multiple_of(2 * inner + j * 128, 128), 128)] = tn(chance, grad2).astype(BF16)

    def pair_grads(place, j, inputs):
        for part in range(3):
            lanes = pl.ds(pl.multiple_of(part * inner + j * 128, 128), 128)
            grads[place, width * part : width * part + width, :] = nn(inputs[part][...], work[:, lanes])

    sqkv_loads = [load(14 + j, sqkv_hbm.at[j], qkv.at[j]) for j in range(pairs)]
    sprob_loads = [load(17 + j, sprob_hbm.at[j], prob.at[j]) for j in range(pairs)]
    for j in range(pairs):
        cqkv_loads[j].wait()
        cprob_loads[j].wait()
        each_item(functools.partial(pair_back, j), 0, middle)
        tick(clock + 1)
        each_item(functools.partial(pair_back, j), middle, items)
        pair_grads(base + 1 + j, j, (first_t, second_t, second_t))
        clock += 2
        tick(clock)
        sqkv_loads[j].start()
        sprob_loads[j].start()
    smix_load = load(20, smix_hbm, mix)
    smix_load.start()
    mid_load.wait()
    text_load.wait()
    smix_load.wait()
    for copy in self_weights:
        copy.wait()
    grads[base + 4] = jnp.zeros_like(grads[base])

    def self_start(i):
        dcross = nt(work[item_rows(i), 0:inner], wqkv[0, :, 0:inner])
        dmem = nt(work[item_rows(i), inner : 3 * inner], wqkv[0, :, inner : 3 * inner])
        emit(i, scaled(dmem).astype(BF16), mem_grad_hbm)
        back, gain_rows = norm_back(xf[i], cross_gain[...], dcross)
        gain_grads[1:2] += gain_rows
        total = din[i] + back
        din[i] = total
        branch = total.astype(BF16)
        dmix[i] = nt(branch, wout[1]).astype(BF16)
        add_out_grad(base + 4, i, branch)
        text = first[i].astype(F32)
        self_in = (text * norm_scale(text) * self_gain[...]).astype(BF16)
        first_t[:, item_rows(i)] = self_in.T

    each_item(self_start, 0, middle)
    tick(clock + 1)
    each_item(self_start, middle, items)
    clock += 2
    tick(clock)
    drain(mem_grad_hbm)
    for j in range(pairs):
        sqkv_loads[j].wait()
        sprob_loads[j].wait()
        each_item(functools.partial(pair_back, j), 0, middle)
        tick(clock + 1)
        each_item(functools.partial(pair_back, j), middle, items)
        pair_grads(base + 5 + j, j, (first_t, first_t, first_t))
        clock += 2
        tick(clock)

    def finish(i):
        dself = nt(work[item_rows(i), :], wqkv[1])
        back, gain_rows = norm_back(first[i].astype(F32), self_gain[...], dself)
        gain_grads[0:1] += gain_rows
        emit(i, scaled(din[i] + back).astype(BF16), text_grad_hbm)

    each_item(finish, 0, middle)
    tick(clock + 1)
    each_item(finish, middle, items)
    clock += 2
    tick(clock)
    drain(text_grad_hbm)
    if linked:
        small[1, 0] = scaled(gain_grads[...])
        small_step(1, 0)
        for step in range(1, max(last_tick - clock, HALVES) + 1):
            if clock + step <= last_tick:
                tick(clock + step)
            if step <= HALVES:
                small_step(1, step)
        gain_grads[...] = small[1, HALVES]
        for k in range(units):
            for copy in result_copies(k):
                copy.wait()


def backward(linked, lengths, group, gains, arrays, shapes):
    items, rows, width, inner, hidden = shapes
    pairs = HEADS // 2
    units = 2 * (hidden // 256) + 2 * (1 + pairs)
    hbm = pl.BlockSpec(memory_space=pl.ANY)
    vmem = pl.BlockSpec(memory_space=pltpu.VMEM)
    smem = pl.BlockSpec(memory_space=pltpu.SMEM)
    row_shape = jax.ShapeDtypeStruct((items, rows, width), BF16)
    gain_shape = jax.ShapeDtypeStruct((8, width), F32)
    grads_shape = (units, 3 * width, 128)
    if linked:
        natural = ([(width, inner)] * 3 + [(inner, width)]) * 2 + [(width, hidden)] * 2 + [(hidden, width)]
        out_shape = [jax.ShapeDtypeStruct(shape, F32) for shape in natural] + [
            gain_shape, jax.ShapeDtypeStruct((8, 128), F32),
        ]
        out_specs = [hbm] * len(natural) + [vmem, vmem]
        scratch = [
            pltpu.VMEM(grads_shape, F32),
            pltpu.VMEM((2, 3 * width, 128), F32),
            pltpu.VMEM((2, HALVES + 1, 8, width), F32),
            pltpu.VMEM((2, HALVES, 8, width), F32),
            pltpu.VMEM((8, 128), F32),
            pltpu.SemaphoreType.DMA((2, LEGS)),
            pltpu.SemaphoreType.DMA((2, LEGS)),
            pltpu.SemaphoreType.DMA((2, HALVES)),
            pltpu.SemaphoreType.DMA((2, HALVES)),
            pltpu.SemaphoreType.DMA((units, 6)),
            pltpu.SemaphoreType.REGULAR((units, HALVES - 1)),
        ]
        params = dict(collective_id=0, has_side_effects=True)
    else:
        out_shape, out_specs = [jax.ShapeDtypeStruct(grads_shape, F32), gain_shape], [vmem, vmem]
        scratch, params = [], {}
    return pl.pallas_call(
        functools.partial(backward_kernel, linked, items, rows, width, inner, hidden),
        in_specs=[smem, smem, vmem, vmem, vmem] + [hbm] * len(arrays),
        out_specs=[hbm, hbm, hbm] + out_specs,
        out_shape=[row_shape, row_shape, row_shape] + out_shape,
        scratch_shapes=scratch + [
            pltpu.VMEM((items, rows, width), F32),
            pltpu.VMEM((items, rows, width), F32),
            pltpu.VMEM((items, rows, width), BF16),
            pltpu.VMEM((items, rows, width), BF16),
            pltpu.VMEM((width, items * rows), BF16),
            pltpu.VMEM((width, items * rows), BF16),
            pltpu.VMEM((width, hidden), BF16),
            pltpu.VMEM((width, hidden), BF16),
            pltpu.VMEM((hidden, width), BF16),
            pltpu.VMEM((items * rows, 3 * inner), BF16),
            pltpu.VMEM((2, width, 3 * inner), BF16),
            pltpu.VMEM((2, inner, width), BF16),
            pltpu.VMEM((pairs, items, rows, 384), BF16),
            pltpu.VMEM((pairs, items, 2 * rows, rows), BF16),
            pltpu.VMEM((items, rows, inner), BF16),
            pltpu.VMEM((items, rows, inner), BF16),
            pltpu.VMEM((2, rows, width), BF16),
            pltpu.SemaphoreType.DMA((21 + items,)),
            pltpu.SemaphoreType.DMA((2,)),
        ],
        compiler_params=pltpu.CompilerParams(vmem_limit_bytes=63 * MIB, **params),
        name="backward",
    )(lengths, group, *gains, *arrays)


def unpack_blocks(width, inner, hidden):
    pairs = HEADS // 2
    blocks = []
    for b in range(hidden // 128):
        blocks.append((8, 0, 128 * b, b, 0, width))
        blocks.append((9, 0, 128 * b, b, width, width))
        for m in range(width // 128):
            blocks.append((10, 128 * b, 128 * m, b, 2 * width + 128 * m, 128))
    base = hidden // 128
    for first_out, start in ((4, base), (0, base + 1 + pairs)):
        for m in range(width // 128):
            blocks.append((first_out + 3, 0, 128 * m, start, inner * m, inner))
        for j in range(pairs):
            for part in range(3):
                blocks.append((first_out + part, 0, 128 * j, start + 1 + j, width * part, width))
    return blocks


def unpack(grads, width, inner, hidden):
    shapes = ([(width, inner)] * 3 + [(inner, width)]) * 2 + [(width, hidden)] * 2 + [(hidden, width)]
    outs = [jnp.zeros(shape, F32) for shape in shapes]
    for out, row, col, unit, start, rows in unpack_blocks(width, inner, hidden):
        outs[out] = outs[out].at[row : row + rows, col : col + 128].set(grads[unit, start : start + rows])
    return outs


def body(
    linked, text_tokens, memory, cotangent, lengths, memory_mask, group_table, self_gain, cross_gain, ffn_gain,
    self_query, self_key, self_value, self_out, cross_query, cross_key, cross_value, cross_out,
    ffn_gate, ffn_up, ffn_down,
):
    items, rows, width = text_tokens.shape
    inner, hidden = self_query.shape[1], ffn_gate.shape[1]
    gains = [gain.reshape(1, width) for gain in (self_gain, cross_gain, ffn_gain)]
    self_weights = [self_query, self_key, self_value, self_out]
    cross_weights = [cross_query, cross_key, cross_value, cross_out]
    sqkv, sprob, smix, mid, cin, cqkv, cprob, cmix, post, fin = forward(
        lengths, text_tokens, memory, memory_mask, gains, self_weights + cross_weights
    )
    arrays = (
        [fin, cotangent, ffn_gate, ffn_up, ffn_down, post, cqkv, cprob, cmix]
        + cross_weights
        + [cin, memory, mid, sqkv, sprob, smix]
        + self_weights
        + [text_tokens]
    )
    shapes = (items, rows, width, inner, hidden)
    if linked:
        layer_output, text_grad, memory_grad, *outs, gain_grads, counts = backward(
            True, lengths, group_table, gains, arrays, shapes
        )
        counts = counts[0, :GROUPS]
    else:
        places = jnp.arange(group_table.shape[0], dtype=jnp.int32)
        own_group = jnp.sum(jnp.where(places == lax.axis_index("wide"), group_table, 0))
        one_hot = (jnp.arange(GROUPS, dtype=jnp.int32) == own_group).astype(F32)
        counts = lax.psum(one_hot * jnp.sum(lengths).astype(F32), AXES)
        root_counts = jnp.sqrt(counts)
        factor = jnp.sum(one_hot * (jnp.sum(counts) / (jnp.sum(root_counts) * root_counts)))
        layer_output, text_grad, memory_grad, grads, gain_grads = backward(
            False, lengths, factor.reshape(1), gains, arrays, shapes
        )
        outs = unpack(lax.psum(factor * grads, AXES), width, inner, hidden)
        gain_grads = lax.psum(factor * gain_grads, AXES)
    return (
        layer_output, text_grad, memory_grad, gain_grads[0], gain_grads[1], gain_grads[2], *outs, counts,
    )


def solution(mesh):
    split, split2, split3, copied = P(AXES), P(AXES, None), P(AXES, None, None), P()
    linked = mesh.shape["wide"] == 8 and mesh.shape["narrow"] == 4
    return jax.shard_map(
        functools.partial(body, linked),
        mesh=mesh,
        in_specs=(split3, split3, split3, split, split2) + (copied,) * 15,
        out_specs=(split3, split3, split3) + (copied,) * 15,
        check_vma=False,
    )
```

time: 1100 us -> 236 us (0.21)
  blocking collectives: 441 us -> 0 us
  matrix products: 284 us -> 0 us
  waiting for transfers between devices: 247 us -> 0 us
  Pallas kernels: 0 us -> 211 us
  local copies, waits for them, and re-layouts: 72.8 us -> 22.9 us
  other arithmetic: 34 us -> 0 us
  between operations: 15 us -> 0.69 us
    all_gather x8 -> x0, blocking collectives: 320 us -> none  [the longest x1 43.9 us: body(): lax.all_gather(shares[10], ('wide', 'narrow'), axis=0, tiled=True)]
    dot_general x45 -> x0, matrix products: 284 us -> none  [the longest x2 48.6 us: attend_backward(): jnp.einsum('ihqk,iqhe->ikhe', score_grad, query_heads, preferred_element_...]
    unnamed x5 -> x0, waiting for transfers between devices: 247 us -> none
    pallas_call x0 -> x2, Pallas kernels: none -> 211 us  [the longest x1 179 us: backward(): pl.pallas_call(functools.partial(backward_kernel, linked, items, rows, wi...]
    unnamed x2 -> x0, blocking collectives: 79.5 us -> none
    psum x1 -> x0, blocking collectives: 42 us -> none  [body(): counts = lax.psum(one_hot * jnp.sum(valid_mask), ('wide', 'narrow'))]
    convert_element_type x8 -> x0, local copies, waits for them, and re-layouts: 20.8 us -> none  [the longest x2 5.34 us: attend_backward(): mixture_grad = split_heads(mixture_grad.astype(jnp.bfloat16))]
    reduce_sum x7 -> x0, other arithmetic: 20.5 us -> none  [the longest x2 12.5 us: attend_forward(): totals = jnp.sum(expo_terms, axis=-1, keepdims=True)]
  transfers between devices with their start and end apart: 4 -> 0, of which waited for: 1 -> 0; matrix products, arithmetic and copies ran while one was open for 5% -> 0% of each run, Pallas kernels for 0% -> 0%
where the time goes in v1:
time: 236 us; the launch traced here: 235 us
  Pallas kernels  211 us (89%)
  local copies, waits for them, and re-layouts  22.9 us (10%)
    pallas_call x1, Pallas kernels, backward(): pl.pallas_call(functools.partial(backward_kernel, linked, items, rows, wi...  179 us
    pallas_call x1, Pallas kernels, forward(): pl.pallas_call(forward_kernel, grid=(items,), in_specs=[pl.BlockSpec(memo...  32.8 us
    unnamed x40, local copies, waits for them, and re-layouts  20.3 us

profile of v1, /device:TPU:0, one launch (start us, length us, event | category | flops | bytes accessed | tf_op | source)
XLA Modules:
  0.0 235.1 jit_solution(10597563934353880921)
XLA Ops:
  0.7 32.8 %forward.1 = (bf16[3,8,256,384]{3,2,1,0:T(8,128)(2,1)}, bf16[3,8,512,256]{3,2,1,0:T(8,128)(2,1)}, bf16[8,256,384]{2,1,0:T(8,128)(2,1)}, f32[8,256,512]{2,1,0:T(8...) custom-call(s32[8]{0:T(128)} %len_ref.3, ...), custom_call_target="tpu_custom_call" | custom-call | tf_op jit(solution)/shard_map/forward/pallas_call | solution.py:163
  33.4 178.7 %backward.1 = (bf16[8,256,512]{2,1,0:T(8,128)(2,1)}, bf16[8,256,512]{2,1,0:T(8,128)(2,1)}, bf16[8,256,512]{2,1,0:T(8,128)(2,1)}, f32[512,384]{1,0:T(8,128)}, f32...) custom-call(s32[8]{0:T(128)} %len_ref.3, ...), custom_call_target="tpu_custom_call" | custom-call | tf_op jit(solution)/shard_map/backward/pallas_call | solution.py:646
  212.2 1.2 slice_bitcast_fusion
  213.3 1.4 fusion
  214.7 0.0 copy-start.4
  214.8 3.2 %copy.52 = bf16[8,256,512]{2,1,0:T(8,128)(2,1)} copy(bf16[8,256,512]{2,1,0:T(8,128)(2,1)} %get-tuple-element.91) | data formatting | bytes 4194304
  217.9 0.0 copy-done.4
  217.9 0.0 copy-start.3
  218.0 1.3 copy.53
  219.3 1.0 copy-done.3
  220.3 0.0 copy-start.12
  220.3 0.0 copy-start.11
  220.3 1.3 copy.54
  221.6 0.4 copy-done.12
  222.0 0.0 copy-start.10
  222.0 0.0 copy-start.9
  222.0 0.9 copy.55
  222.9 0.0 copy-done.11
  222.9 0.0 copy-start.8
  222.9 0.9 copy.56
  223.7 0.0 copy-done.10
  223.7 0.0 copy-start.7
  223.7 0.9 copy.57
  224.6 0.0 copy-done.9
  224.6 0.0 copy-start.6
  224.6 0.9 copy.58
  225.5 0.0 copy-done.8
  225.5 0.0 copy-start.5
  225.5 0.9 copy.59
  226.4 0.0 copy-done.7
  226.4 0.0 copy-start.2
  226.4 0.9 copy.60
  227.3 0.0 copy-done.6
  227.3 0.9 copy.61
  228.2 0.0 copy-done.5
  228.2 0.9 copy.62
  229.0 0.0 copy-done.2
  229.1 0.0 copy-start.1
  229.1 1.3 copy.63
  230.4 1.0 copy-done.1
  231.4 0.0 copy-start
  231.4 1.3 copy.64
  232.7 1.0 copy-done
  233.7 1.3 copy.65
Async XLA Ops:
  214.7 3.2 %copy-start.4 = (bf16[8,256,512]{2,1,0:T(8,128)(2,1)S(1)}, bf16[8,256,512]{2,1,0:T(8,128)(2,1)}, u32[]{:S(2)}) copy-start(bf16[8,256,512]{2,1,0:T(8,128)(2,1)} %get-tuple-element.92) | copy-start | bytes 6291460
  217.9 2.3 copy-start.3
  220.3 1.7 copy-start.12
  220.3 2.6 %copy-start.11 = (f32[512,384]{1,0:T(8,128)S(1)}, f32[512,384]{1,0:T(8,128)}, u32[]{:S(2)}) copy-start(f32[512,384]{1,0:T(8,128)} %get-tuple-element.98) | copy-start | bytes 2359300
  222.0 1.8 copy-start.10
  222.0 2.7 %copy-start.9 = (f32[384,512]{1,0:T(8,128)S(1)}, f32[384,512]{1,0:T(8,128)}, u32[]{:S(2)}) copy-start(f32[384,512]{1,0:T(8,128)} %get-tuple-element.100) | copy-start | bytes 2359300
  222.9 2.7 %copy-start.8 = (f32[512,384]{1,0:T(8,128)S(1)}, f32[512,384]{1,0:T(8,128)}, u32[]{:S(2)}) copy-start(f32[512,384]{1,0:T(8,128)} %get-tuple-element.101) | copy-start | bytes 2359300
  223.7 2.7 %copy-start.7 = (f32[512,384]{1,0:T(8,128)S(1)}, f32[512,384]{1,0:T(8,128)}, u32[]{:S(2)}) copy-start(f32[512,384]{1,0:T(8,128)} %get-tuple-element.102) | copy-start | bytes 2359300
  224.6 2.7 %copy-start.6 = (f32[512,384]{1,0:T(8,128)S(1)}, f32[512,384]{1,0:T(8,128)}, u32[]{:S(2)}) copy-start(f32[512,384]{1,0:T(8,128)} %get-tuple-element.103) | copy-start | bytes 2359300
  225.5 2.7 %copy-start.5 = (f32[384,512]{1,0:T(8,128)S(1)}, f32[384,512]{1,0:T(8,128)}, u32[]{:S(2)}) copy-start(f32[384,512]{1,0:T(8,128)} %get-tuple-element.104) | copy-start | bytes 2359300
  226.4 2.6 %copy-start.2 = (f32[512,1024]{1,0:T(8,128)S(1)}, f32[512,1024]{1,0:T(8,128)}, u32[]{:S(2)}) copy-start(f32[512,1024]{1,0:T(8,128)} %get-tuple-element.105) | copy-start | bytes 6291460
  229.1 2.3 copy-start.1
  231.4 2.3 copy-start

commit v2 on v1

v2 whole, which is shorter than its diff:
```python
import functools

import jax
import jax.numpy as jnp
from jax import lax
from jax.experimental import pallas as pl
from jax.experimental.pallas import tpu as pltpu
from jax.sharding import PartitionSpec as P

HEADS = 6
GROUPS = 2
EPSILON = 1e-06
NEGATIVE = -1e30
F32 = jnp.float32
BF16 = jnp.bfloat16
AXES = ("wide", "narrow")
LIMIT = 44
UNROLL = 4
ROOT = 0.7978845608028654
CUBE = 0.044715
MIB = 1 << 20


def contract(left, right, left_dim, right_dim):
    return lax.dot_general(
        left, right, (((left_dim,), (right_dim,)), ((), ())), preferred_element_type=F32
    )


def nn(left, right):
    return contract(left, right, 1, 0)


def nt(left, right):
    return contract(left, right, 1, 1)


def tn(left, right):
    return contract(left, right, 0, 0)


def norm_scale(values):
    return lax.rsqrt(jnp.mean(values * values, axis=-1, keepdims=True) + EPSILON)


def norm_back(values, gain, grad):
    scale = norm_scale(values)
    unit = values * scale
    gain_rows = grad * unit
    dot = jnp.mean(gain_rows * gain, axis=-1, keepdims=True)
    return scale * (grad * gain - unit * dot), jnp.sum(gain_rows, axis=0, keepdims=True)


def low_lanes(rows):
    return lax.broadcasted_iota(jnp.int32, (rows, 128), 1) < 64


def stack_heads(pair, low):
    zero = jnp.zeros_like(pair)
    return jnp.concatenate([jnp.where(low, pair, zero), jnp.where(low, zero, pair)], axis=0)


def spread_heads(turned):
    zero = jnp.zeros_like(turned[:64])
    return jnp.concatenate(
        [jnp.concatenate([turned[:64], zero], axis=0), jnp.concatenate([zero, turned[64:]], axis=0)], axis=1
    )


def join_heads(turned):
    count = turned.shape[1] // 2
    return jnp.concatenate([turned[:64, :count], turned[64:, count:]], axis=0)


def pair_slice(values, index):
    return values[:, 128 * index : 128 * index + 128]


RISE = (0, 1, 3, 5, 7, 9, 11, 13, 15, 16)
HALVES = 5
LEGS = 2 * HALVES - 1


def exchange_plan():
    wide, narrow = lax.axis_index("wide"), lax.axis_index("narrow")
    z, y = wide // 2, wide % 2
    x, core = narrow // 2, narrow % 2
    near, far = z % 2, z // 2
    flip_x = (wide, (1 - x) * 2 + core)
    flip_y = (z * 2 + 1 - y, narrow)
    flip_core = (wide, x * 2 + 1 - core)
    flip_near = ((far * 2 + 1 - near) * 2 + y, narrow)
    flip_far = (((1 - far) * 2 + near) * 2 + y, narrow)

    def choose(first, second):
        return first + core * (second - first)

    first_flip = tuple(choose(a, b) for a, b in zip(flip_x, flip_y))
    third_flip = tuple(choose(b, a) for a, b in zip(flip_x, flip_y))
    bits = (core, choose(x, y), near, choose(y, x), far)
    partners = (flip_core, first_flip, flip_near, third_flip, flip_far)
    plain = (flip_core, flip_x, flip_near, flip_y, flip_far)
    return bits, partners, plain


def attend(query, key, value, mask, keep):
    low = low_lanes(query.shape[0])
    query = (query * 0.125).astype(BF16)
    key = key.astype(BF16)
    value = value.astype(BF16)
    mixed = []
    for j in range(HEADS // 2):
        q, k, v = pair_slice(query, j), pair_slice(key, j), pair_slice(value, j)
        scores = mask(nt(k, stack_heads(q, low)))
        top = jnp.max(scores, axis=0, keepdims=True)
        expo = jnp.exp(scores - top)
        total = jnp.sum(expo, axis=0, keepdims=True)
        prob = (expo * (1.0 / total)).astype(BF16)
        mixed.append(join_heads(nn(v.T, prob)))
        keep(j, q, k, v, prob)
    return jnp.concatenate(mixed, axis=0).astype(BF16)


def layer_kernel(
    linked, items, rows, width, inner, hidden,
    len_ref, group_ref, mask_ref, self_gain, cross_gain, ffn_gain,
    text_hbm, mem_hbm, cot_hbm, sq_hbm, sk_hbm, sv_hbm, so_hbm, cq_hbm, ck_hbm, cv_hbm, co_hbm,
    gate_hbm, up_hbm, down_hbm,
    grads, first, second, output, gain_out, counts_ref,
    sqkv_hbm, sprob_hbm, smix_hbm, mid_hbm, post_hbm,
    *rest,
):
    (xf, din, first_t, second_t, gate, up, down, work, wqkv, wout, qkv, prob, mix, dmix, gain_grads,
     load_sem, save_sem) = rest[:17]
    if linked:
        halves, small, small_in, factor_ref, send_sem, recv_sem, small_send, small_recv, free_sem = rest[17:]
    pairs = HEADS // 2
    chunk = 256
    chunks = hidden // chunk
    low = low_lanes(rows)
    units = 2 * chunks + 2 * (1 + pairs)
    last_tick = 2 * (units - 1) + RISE[-1]
    if linked:
        bits, partners, plain = exchange_plan()
        barrier = pltpu.get_barrier_semaphore()
        for device in (plain[0], plain[1], plain[2], plain[3], plain[4]):
            pl.semaphore_signal(barrier, inc=1, device_id=device, device_id_type=pl.DeviceIdType.MESH)
        pl.semaphore_wait(barrier, len(plain))

    half = 3 * width // 2

    def region(step, own):
        start = 0
        for s in range(step + 1):
            bit = bits[s] if own or s < step else 1 - bits[s]
            start = start + bit * (half >> s)
        return pl.ds(pl.multiple_of(start, 16), half >> step)

    def half_rows(step):
        size = half >> min(step, HALVES - 2)
        return pl.ds(2 * half - (2 * half >> step), size)

    def stage_copy(index, k):
        slot = k % 2 if isinstance(k, int) else lax.rem(k, 2)
        if index < HALVES:
            sent = region(index, False) if index < HALVES - 1 else region(HALVES - 2, True)
            source, target = grads.at[k, sent], halves.at[slot, half_rows(index)]
            step = index
        else:
            step = LEGS - 1 - index
            source = target = grads.at[k, region(step, True)]
        return pltpu.make_async_remote_copy(
            src_ref=source, dst_ref=target, send_sem=send_sem.at[slot, index], recv_sem=recv_sem.at[slot, index],
            device_id=partners[step], device_id_type=pl.DeviceIdType.MESH,
        )

    def advance(index, k):
        slot = k % 2 if isinstance(k, int) else lax.rem(k, 2)
        if index > 0:
            stage_copy(index - 1, k).wait()
        if 0 < index <= HALVES:
            step = min(index - 1, HALVES - 2)
            own = region(step, True)
            value = grads[k, own, :] + halves[slot, half_rows(index - 1), :]
            if index == 1:
                value = value * factor_ref[0:1, :]
            grads[k, own, :] = value
            if index < HALVES:
                pl.semaphore_signal(
                    free_sem.at[k, step], inc=1, device_id=partners[step], device_id_type=pl.DeviceIdType.MESH
                )
        if index < LEGS:
            if index >= HALVES:
                pl.semaphore_wait(free_sem.at[k, LEGS - 1 - index], 1)
            stage_copy(index, k).start()

    def tick(t):
        if not linked:
            return
        for index in reversed(range(LEGS + 1)):
            u = t - RISE[index]
            if isinstance(t, int):
                if u >= 0 and u % 2 == 0 and u < 2 * units:
                    advance(index, u // 2)
            else:
                ready = (u >= 0) & (u < 2 * units) & (lax.rem(u + 32, 2) == 0)
                pl.when(ready)(functools.partial(advance, index, u // 2))

    def small_copy(use, step):
        return pltpu.make_async_remote_copy(
            src_ref=small.at[use, step], dst_ref=small_in.at[use, step],
            send_sem=small_send.at[use, step], recv_sem=small_recv.at[use, step],
            device_id=plain[step], device_id_type=pl.DeviceIdType.MESH,
        )

    def small_step(use, step):
        if not linked:
            return
        if step > 0:
            small_copy(use, step - 1).wait()
            small[use, step] = small[use, step - 1] + small_in[use, step - 1]
        if step < HALVES:
            small_copy(use, step).start()

    if linked:
        total = len_ref[0]
        for i in range(1, items):
            total = total + len_ref[i]
        lane = lax.broadcasted_iota(jnp.int32, (8, width), 1)
        small[0, 0] = jnp.where(lane == group_ref[lax.axis_index("wide")], total.astype(F32), 0.0)
        small_step(0, 0)

    def set_factor():
        if not linked:
            return
        counts = small[0, HALVES]
        lane = lax.broadcasted_iota(jnp.int32, (8, width), 1)
        counts_ref[...] = counts[:, 0:128]
        roots = jnp.sqrt(counts)
        own = jnp.sum(jnp.where(lane == group_ref[lax.axis_index("wide")], roots, 0.0), axis=-1, keepdims=True)
        top = jnp.sum(counts, axis=-1, keepdims=True)
        bottom = jnp.sum(roots, axis=-1, keepdims=True) * own
        factor_ref[...] = jnp.broadcast_to(top / bottom, (8, 128))

    def scaled(values):
        if linked:
            return values * factor_ref[0:1, 0:1]
        return values * group_ref[0]

    def item_rows(i):
        return pl.ds(pl.multiple_of(i * rows, rows), rows)

    def each_item(body, *marks):
        several(items, body, *marks)

    def several(count, body, *marks):
        def step(i, carry):
            body(i)
            for place, time in marks:
                pl.when(i == place)(functools.partial(tick, time))
            return carry

        lax.fori_loop(0, count, step, 0)

    def load(index, source, target):
        return pltpu.make_async_copy(source, target, load_sem.at[index])

    def weights(base, which, query, key, value, out):
        return [
            load(base, query, wqkv.at[which, :, pl.ds(0, inner)]),
            load(base + 1, key, wqkv.at[which, :, pl.ds(inner, inner)]),
            load(base + 2, value, wqkv.at[which, :, pl.ds(2 * inner, inner)]),
            load(base + 3, out, wout.at[which]),
        ]

    middle = items // 2 - 1
    final = items - 1
    self_weights = weights(0, 1, sq_hbm, sk_hbm, sv_hbm, so_hbm)
    cross_weights = weights(4, 0, cq_hbm, ck_hbm, cv_hbm, co_hbm)
    ffn_loads = [load(8, gate_hbm, gate), load(9, up_hbm, up), load(10, down_hbm, down)]
    text_again = load(11, text_hbm, first)
    smix_load = load(12, smix_hbm, mix)

    def pair_loads(j):
        return [load(13 + j, sqkv_hbm.at[j], qkv.at[j]), load(13 + pairs + j, sprob_hbm.at[j], prob.at[j])]

    lists = 13 + 2 * pairs

    def text_load(i):
        return load(lists + i, text_hbm.at[i], first.at[i])

    def mem_load(i):
        return load(lists + items + i, mem_hbm.at[i], second.at[i])

    def cot_load(i):
        return load(lists + 2 * items + i, cot_hbm.at[i], second.at[i])

    def mem_again(i):
        return load(lists + 3 * items + i, mem_hbm.at[i], work.at[item_rows(i), pl.ds(0, width)])

    def mid_save(i):
        return load(lists + 4 * items + i, din.at[i], mid_hbm.at[i])

    def post_save(i):
        return load(lists + 5 * items + i, xf.at[i], post_hbm.at[i])

    def post_load(i):
        return load(lists + 6 * items + i, post_hbm.at[i], xf.at[i])

    def mid_load(i):
        return load(lists + 7 * items + i, mid_hbm.at[i], xf.at[i])

    for copy in self_weights:
        copy.start()
    for i in range(items):
        text_load(i).start()
    for copy in cross_weights:
        copy.start()
    for i in range(items):
        mem_load(i).start()
    for copy in ffn_loads:
        copy.start()
    gain_grads[...] = jnp.zeros_like(gain_grads)

    def prob_stage(u, j):
        return work.at[pl.ds(rows * (pairs * u + j), rows), pl.ds(0, 2 * rows)]

    def qkv_stage(u, j):
        return work.at[pl.ds(rows * (pairs * u + j), rows), pl.ds(2 * rows, 384)]

    def mix_stage(u):
        return work.at[pl.ds(2 * rows * pairs, inner), pl.ds(rows * u, rows)]

    def saves(u, i):
        copies = [pltpu.make_async_copy(mix_stage(u), smix_hbm.at[i], save_sem.at[u, 0])]
        for j in range(pairs):
            copies.append(pltpu.make_async_copy(qkv_stage(u, j), sqkv_hbm.at[j, i], save_sem.at[u, 1 + j]))
            copies.append(pltpu.make_async_copy(prob_stage(u, j), sprob_hbm.at[j, i], save_sem.at[u, 1 + pairs + j]))
        return copies

    for copy in self_weights:
        copy.wait()
    row = lax.broadcasted_iota(jnp.int32, (rows, 2 * rows), 0)
    col = lax.broadcasted_iota(jnp.int32, (rows, 2 * rows), 1)
    causal = row <= jnp.where(col >= rows, col - rows, col)
    turned_mask = mask_ref[...].astype(F32).T
    item_lane = lax.broadcasted_iota(jnp.int32, (rows, items), 1)

    def forward_two(b, carry):
        numbers = (2 * b, 2 * b + 1)

        @pl.when(b > 0)
        def _():
            for u in range(2):
                for copy in saves(u, 2 * b - 2 + u):
                    copy.wait()

        for i in numbers:
            text_load(i).wait()
        text = first[pl.ds(2 * b, 2)].reshape(2 * rows, width).astype(F32)
        self_in = (text * norm_scale(text) * self_gain[...]).astype(BF16)
        proj = nn(self_in, wqkv[1])
        mixed = []
        for u, i in enumerate(numbers):
            allowed = causal & (row < len_ref[i])
            mine = proj[u * rows : u * rows + rows]

            def keep(j, q, k, v, chance):
                qkv_stage(u, j)[:, 0:128] = q
                qkv_stage(u, j)[:, 128:256] = k
                qkv_stage(u, j)[:, 256:384] = v
                prob_stage(u, j)[...] = chance

            mixed.append(
                attend(
                    mine[:, :inner], mine[:, inner : 2 * inner], mine[:, 2 * inner :],
                    lambda s: jnp.where(allowed, s, NEGATIVE), keep,
                )
            )
            mix_stage(u)[...] = mixed[u]
            for copy in saves(u, i):
                copy.start()

        @pl.when(b == 0)
        def _():
            for copy in cross_weights:
                copy.wait()

        mid = text + tn(jnp.concatenate(mixed, axis=1), wout[1])
        din[pl.ds(2 * b, 2)] = mid.reshape(2, rows, width)
        for i in numbers:
            mid_save(i).start()
        cross_in = (mid * norm_scale(mid) * cross_gain[...]).astype(BF16)
        output[pl.ds(2 * b, 2)] = cross_in.reshape(2, rows, width)
        query = nn(cross_in, wqkv[0, :, 0:inner])
        for i in numbers:
            mem_load(i).wait()
        proj = nn(second[pl.ds(2 * b, 2)].reshape(2 * rows, width), wqkv[0, :, inner : 3 * inner])
        mixed = []
        for u, i in enumerate(numbers):
            cot_load(i).start()
            open_keys = jnp.sum(jnp.where(item_lane == i, turned_mask, 0.0), axis=-1, keepdims=True) > 0.0
            mine = proj[u * rows : u * rows + rows]

            def keep(j, q, k, v, chance):
                qkv[j, i, :, 0:128] = q
                qkv[j, i, :, 128:256] = k
                qkv[j, i, :, 256:384] = v
                prob[j, i] = chance

            mixed.append(
                attend(
                    query[u * rows : u * rows + rows], mine[:, :inner], mine[:, inner:],
                    lambda s: jnp.where(open_keys, s, NEGATIVE), keep,
                )
            )
            mix[i] = mixed[u]
        post = mid + tn(jnp.concatenate(mixed, axis=1), wout[0])
        xf[pl.ds(2 * b, 2)] = post.reshape(2, rows, width)
        for i in numbers:
            post_save(i).start()
        ffn_in = (post * norm_scale(post) * ffn_gain[...]).astype(BF16)
        first[pl.ds(2 * b, 2)] = ffn_in.reshape(2, rows, width)
        first_t[:, pl.ds(pl.multiple_of(2 * b * rows, 2 * rows), 2 * rows)] = ffn_in.T
        for s in range(1, HALVES):
            pl.when(b == s - 1)(functools.partial(small_step, 0, s))
        return carry

    lax.fori_loop(0, items // 2, forward_two, 0)
    for u in range(2):
        for copy in saves(u, items - 2 + u):
            copy.wait()

    def prepare(i):
        cot_load(i).wait()
        row = lax.broadcasted_iota(jnp.int32, (rows, width), 0)
        masked = jnp.where(row < len_ref[i], second[i], jnp.zeros((), BF16))
        second[i] = masked
        second_t[:, item_rows(i)] = masked.T
        mid_save(i).wait()
        post_save(i).wait()

    each_item(prepare)
    for copy in ffn_loads:
        copy.wait()
    small_step(0, HALVES)
    set_factor()

    def ffn_parts(c):
        cols = pl.ds(pl.multiple_of(c * chunk, chunk), chunk)
        return gate.at[:, cols], up.at[:, cols], down.at[cols, :]

    def ffn_grads(c):
        both = nn(first_t[...], work[:, 0 : 2 * chunk])
        turned = nn(second_t[...], work[:, 2 * chunk : 3 * chunk])
        for h in range(chunk // 128):
            place = (chunk // 128) * c + h
            grads[place, 0:width, :] = pair_slice(both, h)
            grads[place, width : 2 * width, :] = pair_slice(both, chunk // 128 + h)
            for m in range(width // 128):
                grads[place, 2 * width + 128 * m : 2 * width + 128 * m + 128, :] = (
                    turned[128 * m : 128 * m + 128, 128 * h : 128 * h + 128].T
                )

    def ffn_front(c):
        wg, wu, wd = ffn_parts(c)

        def elementwise(i):
            source = first[i]
            g = nn(source, wg[...])
            u = nn(source, wu[...])
            dh = nt(second[i], wd[...])
            square = g * g
            t = jnp.tanh(g * (ROOT + (ROOT * CUBE) * square))
            cdf = 0.5 + 0.5 * t
            act = g * cdf
            slope = cdf + 0.5 * g * (1.0 - t * t) * (ROOT + (3.0 * ROOT * CUBE) * square)
            work[item_rows(i), 0:chunk] = (dh * u * slope).astype(BF16)
            work[item_rows(i), chunk : 2 * chunk] = (dh * act).astype(BF16)
            work[item_rows(i), 2 * chunk : 3 * chunk] = (act * u).astype(BF16)

        each_item(elementwise, (middle, 4 * c - 1))
        ffn_grads(c)
        tick(4 * c)

    def back_part(c, i):
        wg, wu, wd = ffn_parts(c)
        return nt(work[item_rows(i), 0:chunk], wg[...]) + nt(work[item_rows(i), chunk : 2 * chunk], wu[...])

    def out_part(c, i):
        wg, wu, wd = ffn_parts(c)
        return xf[i] + nn(work[item_rows(i), 2 * chunk : 3 * chunk], wd[...])

    def ffn_chunk(c, carry):
        ffn_front(c)

        def spread(i):
            xf[i] = out_part(c, i)
            din[i] = jnp.where(c == 0, 0.0, din[i]) + back_part(c, i)

        each_item(spread, (middle, 4 * c + 1), (final, 4 * c + 2))
        return carry

    lax.fori_loop(0, chunks - 1, ffn_chunk, 0)
    ffn_front(chunks - 1)
    text_again.start()
    clock = 4 * (chunks - 1)

    def spread_last(i):
        din[i] += back_part(chunks - 1, i)
        done = out_part(chunks - 1, i).astype(BF16)
        first_t[:, item_rows(i)] = output[i].T
        output[i] = done
        post_load(i).start()
        mem_again(i).start()

    each_item(spread_last, (middle, clock + 1), (final, clock + 2))
    clock += 2

    def add_out_grad(place, i, branch):
        product = nn(mix[i], branch)
        for m in range(width // 128):
            grads[place, inner * m : inner * m + inner, :] += pair_slice(product, m)

    base = 2 * chunks
    grads[base] = jnp.zeros((3 * width, 128), F32)

    def cross_start(i):
        post_load(i).wait()
        back, gain_rows = norm_back(xf[i], ffn_gain[...], din[i])
        mid_load(i).start()
        gain_grads[2:3] += gain_rows
        total = second[i].astype(F32) + back
        din[i] = total
        branch = total.astype(BF16)
        dmix[i] = nt(wout[0], branch).astype(BF16)
        add_out_grad(base, i, branch)
        mem_again(i).wait()
        second_t[:, item_rows(i)] = work[item_rows(i), 0:width].T

    each_item(cross_start, (middle, clock + 1), (final, clock + 2))
    clock += 2

    def pair_terms(j, i):
        lanes = pl.ds(pl.multiple_of(j * 128, 128), 128)
        q, k, v = qkv[j, i, :, 0:128], qkv[j, i, :, 128:256], qkv[j, i, :, 256:384]
        return q, k, v, prob[j, i], dmix[i, lanes, :], mix[i, lanes, :]

    def pair_math(q, k, v, chance, grad, mixed):
        product = grad.astype(F32) * mixed.astype(F32)
        sums = jnp.concatenate(
            [jnp.sum(product[:64], axis=0, keepdims=True), jnp.sum(product[64:], axis=0, keepdims=True)], axis=1
        )
        grad2 = spread_heads(grad)
        score_grad = (chance.astype(F32) * (nn(v, grad2) - sums)).astype(BF16)
        dq = join_heads(nn(k.T, score_grad)) * 0.125
        dk = nn(score_grad, stack_heads(q, low))
        dv = nt(chance, grad2)
        return dq.astype(BF16).T, dk.astype(BF16), dv.astype(BF16)

    def pair_back(j, b):
        numbers = [UNROLL * b + u for u in range(UNROLL)]
        terms = [pair_terms(j, i) for i in numbers]
        made = [pair_math(*entry) for entry in terms]
        for i, entry in zip(numbers, made):
            for part in range(3):
                lanes = pl.ds(pl.multiple_of(part * inner + j * 128, 128), 128)
                work[item_rows(i), lanes] = entry[part]

    def pair_grads(place, j, inputs):
        for part in range(3):
            lanes = pl.ds(pl.multiple_of(part * inner + j * 128, 128), 128)
            grads[place, width * part : width * part + width, :] = nn(inputs[part][...], work[:, lanes])

    def cross_pair(j, carry):
        several(items // UNROLL, functools.partial(pair_back, j), (items // UNROLL // 2 - 1, clock + 1 + 2 * j))
        pair_grads(base + 1 + j, j, (first_t, second_t, second_t))
        for copy in pair_loads(j):
            copy.start()
        tick(clock + 2 + 2 * j)
        return carry

    lax.fori_loop(0, pairs, cross_pair, 0)
    clock += 2 * pairs
    smix_load.start()
    text_again.wait()
    smix_load.wait()
    grads[base + 1 + pairs] = jnp.zeros((3 * width, 128), F32)

    def self_start(i):
        dcross = nt(work[item_rows(i), 0:inner], wqkv[0, :, 0:inner])
        dmem = nt(work[item_rows(i), inner : 3 * inner], wqkv[0, :, inner : 3 * inner])
        second[i] = scaled(dmem).astype(BF16)
        mid_load(i).wait()
        back, gain_rows = norm_back(xf[i], cross_gain[...], dcross)
        gain_grads[1:2] += gain_rows
        total = din[i] + back
        din[i] = total
        branch = total.astype(BF16)
        dmix[i] = nt(wout[1], branch).astype(BF16)
        add_out_grad(base + 1 + pairs, i, branch)
        text = first[i].astype(F32)
        self_in = (text * norm_scale(text) * self_gain[...]).astype(BF16)
        first_t[:, item_rows(i)] = self_in.T

    each_item(self_start, (middle, clock + 1), (final, clock + 2))
    clock += 2

    def self_pair(j, carry):
        for copy in pair_loads(j):
            copy.wait()
        several(items // UNROLL, functools.partial(pair_back, j), (items // UNROLL // 2 - 1, clock + 1 + 2 * j))
        pair_grads(base + 2 + pairs + j, j, (first_t, first_t, first_t))
        tick(clock + 2 + 2 * j)
        return carry

    lax.fori_loop(0, pairs, self_pair, 0)
    clock += 2 * pairs

    def finish(i):
        dself = nt(work[item_rows(i), :], wqkv[1])
        back, gain_rows = norm_back(first[i].astype(F32), self_gain[...], dself)
        gain_grads[0:1] += gain_rows
        first[i] = scaled(din[i] + back).astype(BF16)

    each_item(finish, (middle, clock + 1), (final, clock + 2))
    clock += 2
    if linked:
        small[1, 0] = scaled(gain_grads[...])
        small_step(1, 0)
        for step in range(1, max(last_tick - clock, HALVES) + 1):
            if clock + step <= last_tick:
                tick(clock + step)
            if step <= HALVES:
                small_step(1, step)
        gain_out[...] = small[1, HALVES]
    else:
        gain_out[...] = gain_grads[...]
        counts_ref[...] = jnp.zeros_like(counts_ref)


def run_layer(linked, lengths, group, mask, gains, arrays, shapes):
    items, rows, width, inner, hidden = shapes
    pairs = HEADS // 2
    units = 2 * (hidden // 256) + 2 * (1 + pairs)
    hbm = pl.BlockSpec(memory_space=pl.ANY)
    vmem = pl.BlockSpec(memory_space=pltpu.VMEM)
    smem = pl.BlockSpec(memory_space=pltpu.SMEM)
    place_in = pltpu.VMEM if linked else jax.ShapeDtypeStruct
    scratch, params = [], {}
    if linked:
        scratch = [
            pltpu.VMEM((2, 3 * width, 128), F32),
            pltpu.VMEM((2, HALVES + 1, 8, width), F32),
            pltpu.VMEM((2, HALVES, 8, width), F32),
            pltpu.VMEM((8, 128), F32),
            pltpu.SemaphoreType.DMA((2, LEGS)),
            pltpu.SemaphoreType.DMA((2, LEGS)),
            pltpu.SemaphoreType.DMA((2, HALVES)),
            pltpu.SemaphoreType.DMA((2, HALVES)),
            pltpu.SemaphoreType.REGULAR((units, HALVES - 1)),
        ]
        params = dict(collective_id=0, has_side_effects=True)
    return pl.pallas_call(
        functools.partial(layer_kernel, linked, items, rows, width, inner, hidden),
        in_specs=[smem, smem, vmem, vmem, vmem, vmem] + [hbm] * len(arrays),
        out_specs=[vmem] * 6 + [hbm] * 5,
        out_shape=[
            place_in((units, 3 * width, 128), F32),
            place_in((items, rows, width), BF16),
            place_in((items, rows, width), BF16),
            place_in((items, rows, width), BF16),
            place_in((8, width), F32),
            place_in((8, 128), F32),
            jax.ShapeDtypeStruct((pairs, items, rows, 384), BF16),
            jax.ShapeDtypeStruct((pairs, items, rows, 2 * rows), BF16),
            jax.ShapeDtypeStruct((items, inner, rows), BF16),
            jax.ShapeDtypeStruct((items, rows, width), F32),
            jax.ShapeDtypeStruct((items, rows, width), F32),
        ],
        scratch_shapes=[
            pltpu.VMEM((items, rows, width), F32),
            pltpu.VMEM((items, rows, width), F32),
            pltpu.VMEM((width, items * rows), BF16),
            pltpu.VMEM((width, items * rows), BF16),
            pltpu.VMEM((width, hidden), BF16),
            pltpu.VMEM((width, hidden), BF16),
            pltpu.VMEM((hidden, width), BF16),
            pltpu.VMEM((items * rows, 3 * inner), BF16),
            pltpu.VMEM((2, width, 3 * inner), BF16),
            pltpu.VMEM((2, inner, width), BF16),
            pltpu.VMEM((pairs, items, rows, 384), BF16),
            pltpu.VMEM((pairs, items, rows, 2 * rows), BF16),
            pltpu.VMEM((items, inner, rows), BF16),
            pltpu.VMEM((items, inner, rows), BF16),
            pltpu.VMEM((8, width), F32),
            pltpu.SemaphoreType.DMA((13 + 2 * pairs + 8 * items,)),
            pltpu.SemaphoreType.DMA((2, 1 + 2 * pairs)),
        ] + scratch,
        compiler_params=pltpu.CompilerParams(vmem_limit_bytes=(LIMIT if linked else 63) * MIB, **params),
        name="layer",
    )(lengths, group, mask, *gains, *arrays)


def unpack_blocks(width, inner, hidden):
    pairs = HEADS // 2
    blocks = []
    for b in range(hidden // 128):
        blocks.append((8, 0, 128 * b, b, 0, width))
        blocks.append((9, 0, 128 * b, b, width, width))
        for m in range(width // 128):
            blocks.append((10, 128 * b, 128 * m, b, 2 * width + 128 * m, 128))
    base = hidden // 128
    for first_out, start in ((4, base), (0, base + 1 + pairs)):
        for m in range(width // 128):
            blocks.append((first_out + 3, 0, 128 * m, start, inner * m, inner))
        for j in range(pairs):
            for part in range(3):
                blocks.append((first_out + part, 0, 128 * j, start + 1 + j, width * part, width))
    return blocks


def unpack(grads, width, inner, hidden):
    shapes = ([(width, inner)] * 3 + [(inner, width)]) * 2 + [(width, hidden)] * 2 + [(hidden, width)]
    outs = [jnp.zeros(shape, F32) for shape in shapes]
    for out, row, col, unit, start, rows in unpack_blocks(width, inner, hidden):
        outs[out] = outs[out].at[row : row + rows, col : col + 128].set(grads[unit, start : start + rows])
    return outs


def place_kernel(blocks, grads, text_grad, memory_grad, output, gains, counts, *refs):
    outs, (gain_outs, count_out, sem) = refs[:-5], (refs[-5:-2], refs[-2], refs[-1])
    copies = [
        pltpu.make_async_copy(
            grads.at[unit, pl.ds(start, rows), :], outs[3 + out].at[pl.ds(row, rows), pl.ds(col, 128)], sem.at[n]
        )
        for n, (out, row, col, unit, start, rows) in enumerate(blocks)
    ]
    for n, source in enumerate((output, text_grad, memory_grad)):
        copies.append(pltpu.make_async_copy(source, outs[n], sem.at[len(blocks) + n]))
    for copy in copies:
        copy.start()
    for n in range(3):
        gain_outs[n][...] = gains[n]
    for n in range(GROUPS):
        count_out[n] = jnp.sum(counts[0:1, n : n + 1])
    for copy in copies:
        copy.wait()


def place(arrays, width, inner, hidden):
    blocks = unpack_blocks(width, inner, hidden)
    rows = arrays[1].shape
    shapes = ([(width, inner)] * 3 + [(inner, width)]) * 2 + [(width, hidden)] * 2 + [(hidden, width)]
    hbm, vmem = pl.BlockSpec(memory_space=pl.ANY), pl.BlockSpec(memory_space=pltpu.VMEM)
    return pl.pallas_call(
        functools.partial(place_kernel, blocks),
        in_specs=[vmem] * 6,
        out_specs=[hbm] * (3 + len(shapes)) + [vmem] * 3 + [pl.BlockSpec(memory_space=pltpu.SMEM)],
        out_shape=[jax.ShapeDtypeStruct(rows, BF16)] * 3
        + [jax.ShapeDtypeStruct(shape, F32) for shape in shapes]
        + [jax.ShapeDtypeStruct((width,), F32)] * 3
        + [jax.ShapeDtypeStruct((GROUPS,), F32)],
        scratch_shapes=[pltpu.SemaphoreType.DMA((len(blocks) + 3,))],
        compiler_params=pltpu.CompilerParams(vmem_limit_bytes=1 * MIB),
        name="place",
    )(*[pltpu.with_memory_space_constraint(array, pltpu.VMEM) for array in arrays])


def body(
    linked, text_tokens, memory, cotangent, lengths, memory_mask, group_table, self_gain, cross_gain, ffn_gain,
    self_query, self_key, self_value, self_out, cross_query, cross_key, cross_value, cross_out,
    ffn_gate, ffn_up, ffn_down,
):
    items, rows, width = text_tokens.shape
    inner, hidden = self_query.shape[1], ffn_gate.shape[1]
    gains = [gain.reshape(1, width) for gain in (self_gain, cross_gain, ffn_gain)]
    arrays = [
        text_tokens, memory, cotangent, self_query, self_key, self_value, self_out, cross_query, cross_key,
        cross_value, cross_out, ffn_gate, ffn_up, ffn_down,
    ]
    shapes = (items, rows, width, inner, hidden)
    if linked:
        made = run_layer(True, lengths, group_table, memory_mask, gains, arrays, shapes)
        layer_output, text_grad, memory_grad, *outs = place(made[:6], width, inner, hidden)
        return (layer_output, text_grad, memory_grad, *outs[-4:-1], *outs[:-4], outs[-1])
    places = jnp.arange(group_table.shape[0], dtype=jnp.int32)
    own_group = jnp.sum(jnp.where(places == lax.axis_index("wide"), group_table, 0))
    one_hot = (jnp.arange(GROUPS, dtype=jnp.int32) == own_group).astype(F32)
    counts = lax.psum(one_hot * jnp.sum(lengths).astype(F32), AXES)
    root_counts = jnp.sqrt(counts)
    factor = jnp.sum(one_hot * (jnp.sum(counts) / (jnp.sum(root_counts) * root_counts)))
    grads, text_grad, memory_grad, layer_output, gain_grads, *unused = run_layer(
        False, lengths, factor.reshape(1), memory_mask, gains, arrays, shapes
    )
    outs = unpack(lax.psum(factor * grads, AXES), width, inner, hidden)
    gain_grads = lax.psum(factor * gain_grads, AXES)
    return (
        layer_output, text_grad, memory_grad, gain_grads[0], gain_grads[1], gain_grads[2], *outs, counts,
    )


def solution(mesh):
    split, split2, split3, copied = P(AXES), P(AXES, None), P(AXES, None, None), P()
    linked = mesh.shape["wide"] == 8 and mesh.shape["narrow"] == 4
    return jax.shard_map(
        functools.partial(body, linked),
        mesh=mesh,
        in_specs=(split3, split3, split3, split, split2) + (copied,) * 15,
        out_specs=(split3, split3, split3) + (copied,) * 15,
        check_vma=False,
    )
```

time: 236 us -> 186 us (0.79)
  Pallas kernels: 211 us -> 185 us
  local copies, waits for them, and re-layouts: 22.9 us -> 0 us
    pallas_call x2, Pallas kernels: 211 us -> 185 us  [the longest x1 177 us: run_layer(): pl.pallas_call(functools.partial(layer_kernel, linked, items, rows, width...]
    unnamed x40 -> x0, local copies, waits for them, and re-layouts: 20.3 us -> none
where the time goes in v2:
time: 186 us
  Pallas kernels  185 us (99%)
    pallas_call x1, Pallas kernels, run_layer(): pl.pallas_call(functools.partial(layer_kernel, linked, items, rows, width...  177 us
    pallas_call x1, Pallas kernels, place(): pl.pallas_call(functools.partial(place_kernel, blocks), in_specs=[vmem] *...  7.75 us

profile of v2, /device:TPU:0, one launch (start us, length us, event | category | flops | bytes accessed | tf_op | source)
XLA Modules:
  0.0 185.6 jit_solution(1019129831199612065)
XLA Ops:
  0.7 177.0 %layer.1 = (f32[16,1536,128]{2,1,0:T(8,128)S(1)}, bf16[8,256,512]{2,1,0:T(8,128)(2,1)S(1)}, bf16[8,256,512]{2,1,0:T(8,128)(2,1)S(1)}, bf16[8,256,512]{2,1,0:T(8,...) custom-call(s32[8]{0:T(128)} %len_ref.1, ...), custom_call_target="tpu_custom_call" | custom-call | tf_op jit(solution)/shard_map/layer/pallas_call | solution.py:664
  177.7 7.8 %place.1 = (bf16[8,256,512]{2,1,0:T(8,128)(2,1)}, bf16[8,256,512]{2,1,0:T(8,128)(2,1)}, bf16[8,256,512]{2,1,0:T(8,128)(2,1)}, f32[512,384]{1,0:T(8,128)}, f32[51...) custom-call(f32[16,1536,128]{2,1,0:T(8,128)S(1)} %get-tuple-element., ...), custom_call_target="tpu_custom_call" | custom-call | tf_op jit(solution)/shard_map/place/pallas_call | solution.py:756
